TPU v7x, 32 devices: a whole 2x2x4 slice. The times are simulated.
32 devices in a mesh: ty: 2 (over x), tx: 16 (over z, y, core).
Axes of the slice: x: 2, y: 2, z: 4, core: 2. Of those that a mesh axis runs over, the one named last changes fastest.
Arguments:
- frame_zero: bfloat16 [32, 2048, 128], P('ty', 'tx'), may hold values from -6 to 6
- frame_one: bfloat16 [32, 2048, 128], P('ty', 'tx'), may hold values from -6 to 6
- offset_whole: int32 [2, 2, 32, 2048], P(None, None, 'ty', 'tx'), may hold values from -4 to 3
- offset_frac: float32 [2, 2, 32, 2048], P(None, None, 'ty', 'tx'), may hold values from 0 to 1
- list_tile: int32 [2, 2, 2, 16], P(None, None, 'ty', 'tx'), may hold values from 0 to 31, as said below
- list_pixel: int32 [2, 2, 2, 128], P(None, None, 'ty', 'tx'), may hold values from 0 to 7
- list_weight: bfloat16 [2, 2, 2, 128], P(None, None, 'ty', 'tx'), may hold values from 0.29882812 to 1
- conv_weight: bfloat16 [9, 256, 128], replicated, may hold values from -0.125 to 0.125
- conv_bias: float32 [128], replicated, may hold values from -3 to 3
- mix_weight: bfloat16 [128, 128], replicated, may hold values from -0.5 to 0.5
- mix_bias: float32 [128], replicated, may hold values from -3 to 3
- out_weight: bfloat16 [128, 2], replicated, may hold values from -0.5 to 0.5
- out_bias: float32 [2], replicated, may hold values from -3 to 3
Outputs:
- flow: float32 [2, 2, 32, 2048], P(None, None, 'ty', 'tx')
Inputs may be any that keep to these rules, and one draw needn't show every extreme that they name: `list_tile`: for each direction and entry, every tile is named as a source by exactly one destination tile.
All inputs are finite; a program needn't handle non-finite values.
Results may differ from a plain program's by a relative error of at most 0.0021.
Values may be sent and summed in bfloat16 or wider, within the bound.
A program may use at most 64 MiB of HBM per device.

v0:
```python
import jax
import jax.numpy as jnp
from jax import lax
from jax.sharding import PartitionSpec as P

POOL = 16
MARGIN = 4
ENTRIES = 2


def padded_2(shard, sides, width):
    for axis, dim in sides:
        size, length = (lax.axis_size(axis), shard.shape[dim])
        up = [(i, (i + 1) % size) for i in range(size - 1)]
        down = [(j, i) for i, j in up]
        last = lax.slice_in_dim(shard, length - width, length, axis=dim)
        initial = lax.slice_in_dim(shard, 0, width, axis=dim)
        before = lax.ppermute(last, axis, up)
        after = lax.ppermute(initial, axis, down)
        shard = jnp.concatenate([before, shard, after], axis=dim)
    return shard


def estimate(padded, weights):
    conv_weight, conv_bias, mix_weight, mix_bias, out_weight, out_bias = weights
    tile_height = padded.shape[0] - 2
    tile_width = padded.shape[1] - 2
    summed = jnp.zeros((tile_height, tile_width, conv_weight.shape[2]), jnp.float32)
    for kernel_tap in range(9):
        shift_down = kernel_tap // 3
        shift_right = kernel_tap % 3
        summed = summed + jnp.dot(
            padded[shift_down : shift_down + tile_height, shift_right : shift_right + tile_width],
            conv_weight[kernel_tap],
            preferred_element_type=jnp.float32,
        )
    hidden = jax.nn.relu(summed + conv_bias).astype(jnp.bfloat16)
    mixed_units = jax.nn.relu(
        jnp.dot(hidden, mix_weight, preferred_element_type=jnp.float32) + mix_bias
    ).astype(jnp.bfloat16)
    return jnp.dot(mixed_units, out_weight, preferred_element_type=jnp.float32) + out_bias


def pool_cells(frames):
    count, row_total, col_total, channels = frames.shape
    blocks = frames.astype(jnp.float32).reshape(
        count, row_total // POOL, POOL, col_total // POOL, POOL, channels
    )
    return (jnp.sum(blocks, axis=(2, 4)) / POOL).astype(jnp.bfloat16)


def on_device(
    frame_zero,
    frame_one,
    offset_whole,
    offset_frac,
    list_tile,
    list_pixel,
    list_weight,
    conv_weight,
    conv_bias,
    mix_weight,
    mix_bias,
    out_weight,
    out_bias,
):
    weights = (conv_weight, conv_bias, mix_weight, mix_bias, out_weight, out_bias)
    tile_height, tile_width, channels = frame_zero.shape
    cell_rows = tile_height // POOL
    cell_cols = tile_width // POOL
    cell_count = cell_rows * cell_cols
    frames = jnp.stack([frame_zero, frame_one])
    coarse = pool_cells(frames)
    everyone = lax.all_gather(
        coarse.reshape(1, 2, cell_count, channels), ("ty", "tx"), axis=0, tiled=True
    )
    positions = jnp.arange(cell_count, dtype=jnp.int32)
    warped_cells = []
    for direction in range(2):
        sources = everyone[:, 1 - direction]
        summed = jnp.zeros((cell_count, channels), jnp.float32)
        for member in range(ENTRIES):
            source_block = lax.dynamic_index_in_dim(
                sources, list_tile[direction, member, 0, 0], 0, keepdims=False
            )
            source_pixel = list_pixel[direction, member].reshape(cell_count)
            weight = list_weight[direction, member].reshape(cell_count)
            matrix = jnp.where(
                source_pixel[:, None] == positions[None, :],
                weight[:, None],
                jnp.zeros((), jnp.bfloat16),
            )
            summed = summed + jnp.dot(matrix, source_block, preferred_element_type=jnp.float32)
        warped_cells.append(summed.astype(jnp.bfloat16).reshape(cell_rows, cell_cols, channels))
    coarse_cat = jnp.concatenate([coarse, jnp.stack(warped_cells)], axis=-1)
    padded_cells = padded_2(coarse_cat, (("ty", 1), ("tx", 2)), 1)
    coarse_flow = jnp.stack([estimate(padded_cells[direction], weights) for direction in range(2)])
    sources_fine = padded_2(frames[::-1], (("ty", 1), ("tx", 2)), MARGIN)
    window_width = tile_width + 2 * MARGIN
    local_row = lax.broadcasted_iota(jnp.int32, (tile_height, tile_width), 0)
    local_col = lax.broadcasted_iota(jnp.int32, (tile_height, tile_width), 1)
    warped_tiles = []
    for direction in range(2):
        flat_source = sources_fine[direction].reshape(-1, channels)
        shift_down = offset_whole[direction, 0]
        across = offset_whole[direction, 1]
        frac_down = offset_frac[direction, 0]
        frac_across = offset_frac[direction, 1]
        base_index = (local_row + shift_down + MARGIN) * window_width + local_col + across + MARGIN
        summed = jnp.zeros((tile_height * tile_width, channels), jnp.float32)
        for corner_row in range(2):
            weight_row = frac_down if corner_row == 1 else 1.0 - frac_down
            for corner_col in range(2):
                weight_col = frac_across if corner_col == 1 else 1.0 - frac_across
                weight = lax.optimization_barrier(
                    (weight_row * weight_col).astype(jnp.bfloat16)
                ).astype(jnp.float32)
                target = (base_index + corner_row * window_width + corner_col).reshape(-1)
                picked = jnp.take(flat_source, target, axis=0)
                summed = summed + weight.reshape(-1, 1) * picked.astype(jnp.float32)
        warped_tiles.append(summed.astype(jnp.bfloat16).reshape(tile_height, tile_width, channels))
    warped_stack = jnp.stack(warped_tiles)
    fine_cat = jnp.concatenate([frames, warped_stack], axis=-1)
    padded_fine = padded_2(fine_cat, (("ty", 1), ("tx", 2)), 1)
    upsampled = jnp.repeat(jnp.repeat(coarse_flow, POOL, axis=1), POOL, axis=2)
    flow_fields = (
        jnp.stack([estimate(padded_fine[direction], weights) for direction in range(2)]) + upsampled
    )
    return flow_fields.transpose(0, 3, 1, 2)


def solution(mesh):
    in_specs = (
        P("ty", "tx", None),
        P("ty", "tx", None),
        P(None, None, "ty", "tx"),
        P(None, None, "ty", "tx"),
        P(None, None, "ty", "tx"),
        P(None, None, "ty", "tx"),
        P(None, None, "ty", "tx"),
        P(),
        P(),
        P(),
        P(),
        P(),
        P(),
    )
    out_specs = P(None, None, "ty", "tx")
    return jax.shard_map(
        on_device, mesh=mesh, in_specs=in_specs, out_specs=out_specs, check_vma=False
    )
```

profile of v0, /device:TPU:0, one launch (start us, length us, event | category | flops | bytes accessed | tf_op | source)
XLA Modules:
  0.0 195.3 jit_solution(8600051485091178757)
XLA Ops:
  7.8 43.6 %all-gather = bf16[64,8,128]{2,1,0:T(8,128)(2,1)S(1)} all-gather(bf16[2,8,128]{2,1,0:T(8,128)(2,1)S(1)} %multiply_convert_fusion), channel_id=2, replica_groups=mesh['ty'=2,'tx'=16] {'ty','tx'}, dimensions={0}, use_global_device_ids=true | all-gather | bytes 135168 | tf_op jit(solution)/shard_map/all_gather | solution.py:74
  57.5 4.5 %collective-permute-start.8 = (bf16[2,1,8,256]{3,2,1,0:T(8,128)(2,1)S(1)}, bf16[2,1,8,256]{3,2,1,0:T(8,128)(2,1)S(1)}, u32[]{:S(2)}, u32[]{:S(2)}) collective-permute-start(bf16[2,1,8,256]{3,2,1,0:T(8,128)(2,1)S(1)} %maximum_maximum_fusion.1), channel_id=1, source_target_pairs={{0,16},{1,17},{2,18},{3,19},{4,20},{5,21},{6,22},{7,23},{8,24},{9,... | collective-permute-start | bytes 24584 | tf_op jit(solution)/shard_map/ppermute | solution.py:18
  64.9 4.6 %collective-permute-start = (bf16[2,4,128,128]{3,2,1,0:T(8,128)(2,1)}, bf16[2,4,128,128]{3,2,1,0:T(8,128)(2,1)S(1)}, u32[]{:S(2)}, u32[]{:S(2)}) collective-permute-start(bf16[2,4,128,128]{3,2,1,0:T(8,128)(2,1)} %slice.285), channel_id=1, source_target_pairs={{0,16},{1,17},{2,18},{3,19},{4,20},{5,21},{6,22},{7,23},{8,24},{9,... | collective-permute-start | bytes 786440 | tf_op jit(solution)/shard_map/ppermute | solution.py:18
  74.4 3.2 %collective-permute-start.10 = (bf16[2,3,1,256]{3,2,1,0:T(2,128)(2,1)S(1)}, bf16[2,3,1,256]{3,2,1,0:T(2,128)(2,1)S(1)}, u32[]{:S(2)}, u32[]{:S(2)}) collective-permute-start(bf16[2,3,1,256]{3,2,1,0:T(2,128)(2,1)S(1)} %get-tuple-element.36), channel_id=1, source_target_pairs={{0,1},{1,2},{2,3},{3,4},{4,5},{5,6},{6,7},{7,8},{8,9},{9,10},{10,1... | collective-permute-start | bytes 9224 | tf_op jit(solution)/shard_map/ppermute | solution.py:18
  85.1 3.0 %collective-permute-start.2 = (bf16[2,24,4,128]{3,2,1,0:T(4,128)(2,1)S(1)}, bf16[2,24,4,128]{3,2,1,0:T(4,128)(2,1)S(1)}, u32[]{:S(2)}, u32[]{:S(2)}) collective-permute-start(bf16[2,24,4,128]{3,2,1,0:T(4,128)(2,1)S(1)} %get-tuple-element.18), channel_id=1, source_target_pairs={{0,1},{1,2},{2,3},{3,4},{4,5},{5,6},{6,7},{7,8},{8,9},{9,10},{10,1... | collective-permute-start | bytes 147464 | tf_op jit(solution)/shard_map/ppermute | solution.py:18
  88.2 1.5 fusion.21
  91.1 8.0 %gather_fusion.7 = bf16[2048,128]{1,0:T(8,128)(2,1)} fusion(bf16[3264,128]{1,0:T(8,128)(2,1)S(1)} %bitcast.349, s32[2048]{0:T(1024)S(1)} %copy-done.10), kind=kCustom, calls=%fused_computation.7.clone | custom fusion | bytes 1056768 | tf_op jit(solution)/shard_map/jit(_take)/gather | solution.py:119
  99.0 8.0 %gather_fusion.6 = bf16[2048,128]{1,0:T(8,128)(2,1)} fusion(bf16[3264,128]{1,0:T(8,128)(2,1)S(1)} %bitcast.350, s32[2048]{0:T(1024)S(1)} %copy-done.7), kind=kCustom, calls=%fused_computation.6.clone | custom fusion | bytes 1056768 | tf_op jit(solution)/shard_map/jit(_take)/gather | solution.py:119
  107.0 8.0 %gather_fusion.5 = bf16[2048,128]{1,0:T(8,128)(2,1)} fusion(bf16[3264,128]{1,0:T(8,128)(2,1)S(1)} %bitcast.351, s32[2048]{0:T(1024)S(1)} %get-tuple-element.67), kind=kCustom, calls=%fused_computation.5.clone | custom fusion | bytes 1056768 | tf_op jit(solution)/shard_map/jit(_take)/gather | solution.py:119
  115.0 8.0 %gather_fusion.4 = bf16[2048,128]{1,0:T(8,128)(2,1)} fusion(bf16[3264,128]{1,0:T(8,128)(2,1)S(1)} %bitcast.352, s32[2048]{0:T(1024)S(1)} %get-tuple-element.70), kind=kCustom, calls=%fused_computation.4.clone | custom fusion | bytes 1056768 | tf_op jit(solution)/shard_map/jit(_take)/gather | solution.py:119
  122.9 6.2 %gather_fusion.3 = bf16[2048,128]{1,0:T(8,128)(2,1)S(1)} fusion(bf16[3264,128]{1,0:T(8,128)(2,1)S(1)} %bitcast.345, s32[2048]{0:T(1024)S(1)} %get-tuple-element.42), kind=kCustom, calls=%fused_computation.3.clone | custom fusion | bytes 1056768 | tf_op jit(solution)/shard_map/jit(_take)/gather | solution.py:119
  129.1 8.0 %gather_fusion.2 = bf16[2048,128]{1,0:T(8,128)(2,1)} fusion(bf16[3264,128]{1,0:T(8,128)(2,1)S(1)} %bitcast.346, s32[2048]{0:T(1024)S(1)} %get-tuple-element.43), kind=kCustom, calls=%fused_computation.2.clone | custom fusion | bytes 1056768 | tf_op jit(solution)/shard_map/jit(_take)/gather | solution.py:119
  137.1 8.0 %gather_fusion.1 = bf16[2048,128]{1,0:T(8,128)(2,1)} fusion(bf16[3264,128]{1,0:T(8,128)(2,1)S(1)} %bitcast.347, s32[2048]{0:T(1024)S(1)} %get-tuple-element.44), kind=kCustom, calls=%fused_computation.1.clone | custom fusion | bytes 1056768 | tf_op jit(solution)/shard_map/jit(_take)/gather | solution.py:119
  145.1 8.0 %gather_fusion = bf16[2048,128]{1,0:T(8,128)(2,1)} fusion(bf16[3264,128]{1,0:T(8,128)(2,1)S(1)} %bitcast.348, s32[2048]{0:T(1024)S(1)} %get-tuple-element.41), kind=kCustom, calls=%fused_computation.clone | custom fusion | bytes 1056768 | tf_op jit(solution)/shard_map/jit(_take)/gather | solution.py:119
  153.2 5.7 %add_convert_fusion = bf16[2048,128]{1,0:T(8,128)(2,1)S(1)} fusion(bf16[2048,128]{1,0:T(8,128)(2,1)} %gather_fusion.7, bf16[2048,128]{1,0:T(8,128)(2,1)} %gather_fusion.6, bf16[2048,128]{1,0:T(8,128)(2,1)} %gather_fusion.5, bf16[2048,128]{1,0:T(8,128)(2,1)} %gather_fusion.4, f32[2048]{0:T(1024)S(1)} %copy-done.11, f32[2048]{0:T(1024)S(1)} %copy-done.12, ...), kind=kLoop, calls=%fused_computation.108 | loop fusion | flops 4194304 | bytes 2662400 | tf_op jit(solution)/shard_map/convert_element_type | solution.py:121
  159.0 2.9 %add_convert_fusion.1 = bf16[2048,128]{1,0:T(8,128)(2,1)S(1)} fusion(bf16[2048,128]{1,0:T(8,128)(2,1)S(1)} %gather_fusion.3, bf16[2048,128]{1,0:T(8,128)(2,1)S(1)} %copy-done.4, bf16[2048,128]{1,0:T(8,128)(2,1)S(1)} %copy-done.5, bf16[2048,128]{1,0:T(8,128)(2,1)S(1)} %copy-done.6, f32[2048]{0:T(1024)S(1)} %get-tuple-element.75, ...), kind=kLoop, calls=%fused_computation.109 | loop fusion | flops 4194304 | bytes 2662400 | tf_op jit(solution)/shard_map/convert_element_type | solution.py:121
  163.3 4.6 %collective-permute-start.4 = (bf16[2,1,128,256]{3,2,1,0:T(8,128)(2,1)S(1)}, bf16[2,1,128,256]{3,2,1,0:T(8,128)(2,1)S(1)}, u32[]{:S(2)}, u32[]{:S(2)}) collective-permute-start(bf16[2,1,128,256]{3,2,1,0:T(8,128)(2,1)S(1)} %get-tuple-element.14), channel_id=1, source_target_pairs={{0,16},{1,17},{2,18},{3,19},{4,20},{5,21},{6,22},{7,23},{8,24},{9,... | collective-permute-start | bytes 393224 | tf_op jit(solution)/shard_map/ppermute | solution.py:18
  168.1 1.5 collective-permute-done.5
  169.6 1.8 collective-permute-done.4
  172.8 3.2 %collective-permute-start.6 = (bf16[2,18,1,256]{3,2,1,0:T(2,128)(2,1)S(1)}, bf16[2,18,1,256]{3,2,1,0:T(2,128)(2,1)S(1)}, u32[]{:S(2)}, u32[]{:S(2)}) collective-permute-start(bf16[2,18,1,256]{3,2,1,0:T(2,128)(2,1)S(1)} %get-tuple-element.12), channel_id=1, source_target_pairs={{0,1},{1,2},{2,3},{3,4},{4,5},{5,6},{6,7},{7,8},{8,9},{9,10},{10,1... | collective-permute-start | bytes 55304 | tf_op jit(solution)/shard_map/ppermute | solution.py:18
  176.7 2.4 %pad_maximum_fusion = bf16[2,18,130,256]{3,2,1,0:T(8,128)(2,1)S(1)} fusion(bf16[2,18,1,256]{3,2,1,0:T(2,128)(2,1)S(1)} %collective-permute-done.7, bf16[2,1,128,256]{3,2,1,0:T(8,128)(2,1)S(1)} %collective-permute-done.5, bf16[1,16,128,128]{3,2,1,0:T(8,128)(2,1)S(1)} %bitcast.367, bf16[1,16,128,128]{3,2,1,0:T(8,128)(2,1)S(1)} %bitcast.370, ...), kind=kLoop, calls=%fused_computation.8 | loop fusion | flops 19169280 | bytes 4792320 | tf_op jit(solution)/shard_map/concatenate | solution.py:20
  182.5 1.5 convolution_add_fusion.1
  184.0 2.8 %fusion.7 = bf16[16,128,128]{2,1,0:T(8,128)(2,1)} fusion(f32[16,128,128]{2,1,0:T(8,128)} %convolution_add_fusion.1, bf16[18,130,256]{2,1,0:T(8,128)(2,1)S(1)} %get-tuple-element.11, f32[128]{0:T(128)S(1)} %copy-done.27, f32[128]{0:T(128)S(1)} %copy-done.29, bf16[9,256,128]{2,1,0:T(8,128)(2,1)S(1)} %copy-done.3, bf16[128,128]{1,0:T(8,128)(2,1)S(1)} %copy-done), kind=kOutput, calls=%fused_computation.41 | convolution fusion | flops 203161600 | bytes 2720768 | tf_op jit(solution)/shard_map/dot_general | solution.py:39
  191.7 1.6 fusion.6
  (159 shorter events, 36.5 us)
Async XLA Ops:
  0.0 82.9 %copy-start = (bf16[128,128]{1,0:T(8,128)(2,1)S(1)}, bf16[128,128]{1,0:T(8,128)(2,1)}, u32[]{:S(2)}) copy-start(bf16[128,128]{1,0:T(8,128)(2,1)} %param.24) | copy-start | bytes 98308
  0.0 62.0 %copy-start.2 = (bf16[16,128,128]{2,1,0:T(8,128)(2,1)S(1)}, bf16[16,128,128]{2,1,0:T(8,128)(2,1)}, u32[]{:S(2)}) copy-start(bf16[16,128,128]{2,1,0:T(8,128)(2,1)} %param.16) | copy-start | bytes 1572868
  0.0 62.0 %copy-start.1 = (bf16[16,128,128]{2,1,0:T(8,128)(2,1)S(1)}, bf16[16,128,128]{2,1,0:T(8,128)(2,1)}, u32[]{:S(2)}) copy-start(bf16[16,128,128]{2,1,0:T(8,128)(2,1)} %param.15) | copy-start | bytes 1572868
  51.4 18.0 %copy-start.16 = (s32[2,2,16,128]{3,2,1,0:T(8,128)S(1)}, s32[2,2,16,128]{3,2,1,0:T(8,128)}, u32[]{:S(2)}) copy-start(s32[2,2,16,128]{3,2,1,0:T(8,128)} %param.17) | copy-start | bytes 98308
  52.2 19.1 %copy-start.15 = (f32[2,2,16,128]{3,2,1,0:T(8,128)S(1)}, f32[2,2,16,128]{3,2,1,0:T(8,128)}, u32[]{:S(2)}) copy-start(f32[2,2,16,128]{3,2,1,0:T(8,128)} %param.18) | copy-start | bytes 98308
  56.2 16.9 %collective-permute-start.9 = (bf16[2,1,8,256]{3,2,1,0:T(8,128)(2,1)S(1)}, bf16[2,1,8,256]{3,2,1,0:T(8,128)(2,1)S(1)}, u32[]{:S(2)}, u32[]{:S(2)}) collective-permute-start(bf16[2,1,8,256]{3,2,1,0:T(8,128)(2,1)S(1)} %maximum_maximum_fusion.1), channel_id=1, source_target_pairs={{16,0},{17,1},{18,2},{19,3},{20,4},{21,5},{22,6},{23,7},{24,8},{25... | collective-permute-start | bytes 24584 | tf_op jit(solution)/shard_map/ppermute | solution.py:19
  57.5 15.6 %collective-permute-start.8 = (bf16[2,1,8,256]{3,2,1,0:T(8,128)(2,1)S(1)}, bf16[2,1,8,256]{3,2,1,0:T(8,128)(2,1)S(1)}, u32[]{:S(2)}, u32[]{:S(2)}) collective-permute-start(bf16[2,1,8,256]{3,2,1,0:T(8,128)(2,1)S(1)} %maximum_maximum_fusion.1), channel_id=1, source_target_pairs={{0,16},{1,17},{2,18},{3,19},{4,20},{5,21},{6,22},{7,23},{8,24},{9,... | collective-permute-start | bytes 24584 | tf_op jit(solution)/shard_map/ppermute | solution.py:18
  62.8 20.9 %collective-permute-start.1 = (bf16[2,4,128,128]{3,2,1,0:T(8,128)(2,1)}, bf16[2,4,128,128]{3,2,1,0:T(8,128)(2,1)S(1)}, u32[]{:S(2)}, u32[]{:S(2)}) collective-permute-start(bf16[2,4,128,128]{3,2,1,0:T(8,128)(2,1)} %slice.287), channel_id=1, source_target_pairs={{16,0},{17,1},{18,2},{19,3},{20,4},{21,5},{22,6},{23,7},{24,8},{25... | collective-permute-start | bytes 786440 | tf_op jit(solution)/shard_map/ppermute | solution.py:19
  64.9 18.9 %collective-permute-start = (bf16[2,4,128,128]{3,2,1,0:T(8,128)(2,1)}, bf16[2,4,128,128]{3,2,1,0:T(8,128)(2,1)S(1)}, u32[]{:S(2)}, u32[]{:S(2)}) collective-permute-start(bf16[2,4,128,128]{3,2,1,0:T(8,128)(2,1)} %slice.285), channel_id=1, source_target_pairs={{0,16},{1,17},{2,18},{3,19},{4,20},{5,21},{6,22},{7,23},{8,24},{9,... | collective-permute-start | bytes 786440 | tf_op jit(solution)/shard_map/ppermute | solution.py:18
  73.1 6.9 %collective-permute-start.11 = (bf16[2,3,1,256]{3,2,1,0:T(2,128)(2,1)S(1)}, bf16[2,3,1,256]{3,2,1,0:T(2,128)(2,1)S(1)}, u32[]{:S(2)}, u32[]{:S(2)}) collective-permute-start(bf16[2,3,1,256]{3,2,1,0:T(2,128)(2,1)S(1)} %get-tuple-element.37), channel_id=1, source_target_pairs={{1,0},{2,1},{3,2},{4,3},{5,4},{6,5},{7,6},{8,7},{9,8},{10,9},{11,1... | collective-permute-start | bytes 9224 | tf_op jit(solution)/shard_map/ppermute | solution.py:19
  74.4 5.6 %collective-permute-start.10 = (bf16[2,3,1,256]{3,2,1,0:T(2,128)(2,1)S(1)}, bf16[2,3,1,256]{3,2,1,0:T(2,128)(2,1)S(1)}, u32[]{:S(2)}, u32[]{:S(2)}) collective-permute-start(bf16[2,3,1,256]{3,2,1,0:T(2,128)(2,1)S(1)} %get-tuple-element.36), channel_id=1, source_target_pairs={{0,1},{1,2},{2,3},{3,4},{4,5},{5,6},{6,7},{7,8},{8,9},{9,10},{10,1... | collective-permute-start | bytes 9224 | tf_op jit(solution)/shard_map/ppermute | solution.py:18
  83.8 5.9 %collective-permute-start.3 = (bf16[2,24,4,128]{3,2,1,0:T(4,128)(2,1)S(1)}, bf16[2,24,4,128]{3,2,1,0:T(4,128)(2,1)S(1)}, u32[]{:S(2)}, u32[]{:S(2)}) collective-permute-start(bf16[2,24,4,128]{3,2,1,0:T(4,128)(2,1)S(1)} %get-tuple-element.19), channel_id=1, source_target_pairs={{1,0},{2,1},{3,2},{4,3},{5,4},{6,5},{7,6},{8,7},{9,8},{10,9},{11,1... | collective-permute-start | bytes 147464 | tf_op jit(solution)/shard_map/ppermute | solution.py:19
  85.1 4.6 %collective-permute-start.2 = (bf16[2,24,4,128]{3,2,1,0:T(4,128)(2,1)S(1)}, bf16[2,24,4,128]{3,2,1,0:T(4,128)(2,1)S(1)}, u32[]{:S(2)}, u32[]{:S(2)}) collective-permute-start(bf16[2,24,4,128]{3,2,1,0:T(4,128)(2,1)S(1)} %get-tuple-element.18), channel_id=1, source_target_pairs={{0,1},{1,2},{2,3},{3,4},{4,5},{5,6},{6,7},{7,8},{8,9},{9,10},{10,1... | collective-permute-start | bytes 147464 | tf_op jit(solution)/shard_map/ppermute | solution.py:18
  145.1 8.1 %copy-start.12 = (f32[2048]{0:T(1024)S(1)}, f32[2048]{0:T(1024)}, u32[]{:S(2)}) copy-start(f32[2048]{0:T(1024)} %get-tuple-element.72) | copy-start | bytes 24580
  145.1 8.1 %copy-start.13 = (f32[2048]{0:T(1024)S(1)}, f32[2048]{0:T(1024)}, u32[]{:S(2)}) copy-start(f32[2048]{0:T(1024)} %get-tuple-element.73) | copy-start | bytes 24580
  145.1 8.1 %copy-start.14 = (f32[2048]{0:T(1024)S(1)}, f32[2048]{0:T(1024)}, u32[]{:S(2)}) copy-start(f32[2048]{0:T(1024)} %get-tuple-element.74) | copy-start | bytes 24580
  145.1 8.1 %copy-start.21 = (pred[2048]{0:T(1024)(128)(4,1)S(1)}, pred[2048]{0:T(1024)(128)(4,1)}, u32[]{:S(2)}) copy-start(pred[2048]{0:T(1024)(128)(4,1)} %get-tuple-element.45) | copy-start | bytes 6148
  145.1 8.1 %copy-start.22 = (pred[2048]{0:T(1024)(128)(4,1)S(1)}, pred[2048]{0:T(1024)(128)(4,1)}, u32[]{:S(2)}) copy-start(pred[2048]{0:T(1024)(128)(4,1)} %get-tuple-element.46) | copy-start | bytes 6148
  145.1 8.1 %copy-start.23 = (pred[2048]{0:T(1024)(128)(4,1)S(1)}, pred[2048]{0:T(1024)(128)(4,1)}, u32[]{:S(2)}) copy-start(pred[2048]{0:T(1024)(128)(4,1)} %get-tuple-element.47) | copy-start | bytes 6148
  145.1 8.1 %copy-start.25 = (pred[2048]{0:T(1024)(128)(4,1)S(1)}, pred[2048]{0:T(1024)(128)(4,1)}, u32[]{:S(2)}) copy-start(pred[2048]{0:T(1024)(128)(4,1)} %get-tuple-element.34) | copy-start | bytes 6148
  162.0 7.6 %collective-permute-start.5 = (bf16[2,1,128,256]{3,2,1,0:T(8,128)(2,1)S(1)}, bf16[2,1,128,256]{3,2,1,0:T(8,128)(2,1)S(1)}, u32[]{:S(2)}, u32[]{:S(2)}) collective-permute-start(bf16[2,1,128,256]{3,2,1,0:T(8,128)(2,1)S(1)} %get-tuple-element.15), channel_id=1, source_target_pairs={{16,0},{17,1},{18,2},{19,3},{20,4},{21,5},{22,6},{23,7},{24,8},{25... | collective-permute-start | bytes 393224 | tf_op jit(solution)/shard_map/ppermute | solution.py:19
  163.3 8.1 %collective-permute-start.4 = (bf16[2,1,128,256]{3,2,1,0:T(8,128)(2,1)S(1)}, bf16[2,1,128,256]{3,2,1,0:T(8,128)(2,1)S(1)}, u32[]{:S(2)}, u32[]{:S(2)}) collective-permute-start(bf16[2,1,128,256]{3,2,1,0:T(8,128)(2,1)S(1)} %get-tuple-element.14), channel_id=1, source_target_pairs={{0,16},{1,17},{2,18},{3,19},{4,20},{5,21},{6,22},{7,23},{8,24},{9,... | collective-permute-start | bytes 393224 | tf_op jit(solution)/shard_map/ppermute | solution.py:18
  171.5 4.7 %collective-permute-start.7 = (bf16[2,18,1,256]{3,2,1,0:T(2,128)(2,1)S(1)}, bf16[2,18,1,256]{3,2,1,0:T(2,128)(2,1)S(1)}, u32[]{:S(2)}, u32[]{:S(2)}) collective-permute-start(bf16[2,18,1,256]{3,2,1,0:T(2,128)(2,1)S(1)} %get-tuple-element.13), channel_id=1, source_target_pairs={{1,0},{2,1},{3,2},{4,3},{5,4},{6,5},{7,6},{8,7},{9,8},{10,9},{11,1... | collective-permute-start | bytes 55304 | tf_op jit(solution)/shard_map/ppermute | solution.py:19
  172.8 3.9 %collective-permute-start.6 = (bf16[2,18,1,256]{3,2,1,0:T(2,128)(2,1)S(1)}, bf16[2,18,1,256]{3,2,1,0:T(2,128)(2,1)S(1)}, u32[]{:S(2)}, u32[]{:S(2)}) collective-permute-start(bf16[2,18,1,256]{3,2,1,0:T(2,128)(2,1)S(1)} %get-tuple-element.12), channel_id=1, source_target_pairs={{0,1},{1,2},{2,3},{3,4},{4,5},{5,6},{6,7},{7,8},{8,9},{9,10},{10,1... | collective-permute-start | bytes 55304 | tf_op jit(solution)/shard_map/ppermute | solution.py:18
  (22 other events, 115.4 us)
where the time goes:
time: 199 us; the launch traced here: 195 us
  local copies, waits for them, and re-layouts  69.3 us (35%)
  blocking collectives  43.6 us (22%)
  starting transfers between devices  30.8 us (15%)
  matrix products  21.2 us (11%)
  other arithmetic  18.2 us (9%)
  between operations  8.32 us (4%)
  waiting for transfers between devices  3.84 us (2%)
    gather x8, local copies, waits for them, and re-layouts, on_device(): picked = jnp.take(flat_source, target, axis=0)  61.9 us
    all_gather x1, blocking collectives, on_device(): lax.all_gather(coarse.reshape(1, 2, cell_count, channels), ('ty', 'tx'),...  43.6 us
    ppermute x6, starting transfers between devices, padded_2(): before = lax.ppermute(last, axis, up)  23.1 us
    dot_general x32, matrix products, estimate(): jnp.dot(padded[shift_down:shift_down + tile_height, shift_right:shift_rig...  11 us
    convert_element_type x2, other arithmetic, on_device(): summed.astype(jnp.bfloat16).reshape(tile_height, tile_width, channels)  8.65 us
    ppermute x6, starting transfers between devices, padded_2(): after = lax.ppermute(initial, axis, down)  7.73 us
    dot_general x4, matrix products, estimate(): jnp.dot(hidden, mix_weight, preferred_element_type=jnp.float32) + mix_bias  6.77 us
  transfers between devices with their start and end apart: 12, of which 3 were waited for; matrix products, arithmetic and copies ran while one was open for 7% of the time, Pallas kernels for 0%

commit v1 on v0

v1 whole, which is shorter than its diff:
```python
import functools

import jax
import jax.numpy as jnp
from jax import lax
from jax.experimental import pallas as pl
from jax.experimental.pallas import tpu as pltpu
from jax.sharding import PartitionSpec as P

POOL = 16
MARGIN = 4
EDGE = 16
DIRS = [(-1, 0), (1, 0), (0, -1), (0, 1), (-1, -1), (-1, 1), (1, -1), (1, 1)]
MESH = pl.DeviceIdType.MESH
BF = jnp.bfloat16
F32 = jnp.float32


def part(step, center, size, margin):
    if step < 0:
        return pl.ds(center - margin, margin)
    if step > 0:
        return pl.ds(center + size, margin)
    return pl.ds(center, size)


def rim(step, start, size, margin):
    if step < 0:
        return pl.ds(start, margin)
    if step > 0:
        return pl.ds(start + size - margin, margin)
    return pl.ds(start, size)


def nt(a, b):
    return lax.dot_general(a, b, (((1,), (1,)), ((), ())), preferred_element_type=F32)


def kernel(
    n_ty, n_tx, height, width,
    f0, f1, whole, frac, index, weight, conv_w, conv_b, mix_w, mix_b, out_w, out_b,
    out,
    F, F4, Wp, X, G, CW, T,
    load_sem, halo_send, halo_recv, all_send, all_recv, rim_send, rim_recv, cell_send, cell_recv,
):
    n = n_ty * n_tx
    ty, tx = lax.axis_index("ty"), lax.axis_index("tx")
    me = ty * n_tx + tx
    frames = (f0, f1)
    cells = width // POOL

    def has(dy, dx):
        return (ty + dy >= 0) & (ty + dy < n_ty) & (tx + dx >= 0) & (tx + dx < n_tx)

    def at(dy, dx):
        return (lax.rem(ty + dy + n_ty, n_ty), lax.rem(tx + dx + n_tx, n_tx))

    loads = [
        pltpu.make_async_copy(
            frames[f], F.at[f, pl.ds(MARGIN, height), pl.ds(EDGE, width)], load_sem.at[f]
        )
        for f in range(2)
    ]
    for load in loads:
        load.start()

    barrier = pltpu.get_barrier_semaphore()

    def greet(k, _):
        other = lax.rem(me + k, n)
        pl.semaphore_signal(
            barrier, inc=1, device_id=(other // n_tx, lax.rem(other, n_tx)), device_id_type=MESH
        )
        return 0

    lax.fori_loop(1, n, greet, 0)

    for dy, dx in DIRS:
        @pl.when(jnp.logical_not(has(dy, dx)))
        def _():
            rows, cols = part(dy, MARGIN, height, MARGIN), part(dx, EDGE, width, EDGE)
            F[:, rows, cols, :] = jnp.zeros((2, rows.size, cols.size, F.shape[3]), BF)
            rows = part(dy, 1, height, 1)
            Wp[:, rows, cols, :] = jnp.zeros((2, rows.size, cols.size, F.shape[3]), BF)

    pl.semaphore_wait(barrier, n - 1)

    def halo(s, f):
        dy, dx = DIRS[s]
        return pltpu.make_async_remote_copy(
            src_ref=frames[f].at[rim(dy, 0, height, MARGIN), rim(dx, 0, width, EDGE)],
            dst_ref=F.at[f, part(-dy, MARGIN, height, MARGIN), part(-dx, EDGE, width, EDGE)],
            send_sem=halo_send.at[s, f],
            recv_sem=halo_recv.at[s, f],
            device_id=at(dy, dx),
            device_id_type=MESH,
        )

    for s, (dy, dx) in enumerate(DIRS):
        @pl.when(has(dy, dx))
        def _():
            for f in range(2):
                halo(s, f).start()

    for load in loads:
        load.wait()
    pooled = []
    for f in range(2):
        def add_row(r, total):
            return total + F[f, MARGIN + r, EDGE : EDGE + width, :].astype(F32)

        total = lax.fori_loop(0, height, add_row, jnp.zeros((width, F.shape[3]), F32))
        pooled.append(jnp.sum(total.reshape(cells, POOL, -1), axis=1) / POOL)
    G[me] = jnp.concatenate(pooled, axis=0).astype(BF)

    def push(k):
        other = lax.rem(me + k, n)
        return pltpu.make_async_remote_copy(
            src_ref=G.at[me],
            dst_ref=G.at[me],
            send_sem=all_send.at[k],
            recv_sem=all_recv.at[k],
            device_id=(other // n_tx, lax.rem(other, n_tx)),
            device_id_type=MESH,
        )

    def push_start(k, _):
        push(k).start()
        return 0

    lax.fori_loop(1, n, push_start, 0)

    lane = lax.broadcasted_iota(jnp.int32, (8, 128), 1)
    pair = lax.broadcasted_iota(jnp.int32, (8, 128), 0)
    lane_row = (lane // 8) % 8
    lane_col = lane % 8
    source_lane = (2 * pair + lane // 64) * 8 + lane_col

    def blocked(rows):
        got = jnp.zeros((8, 128), rows.dtype)
        for r in range(8):
            row = jnp.broadcast_to(rows[r : r + 1, :], (8, 128))
            picked = jnp.take_along_axis(row, source_lane, axis=1, mode="promise_in_bounds")
            got = jnp.where(lane_row == r, picked, got)
        return got

    for d in range(2):
        for band in range(2):
            rows = pl.ds(band * 8, 8)
            a, b = blocked(whole[d, 0, rows, :]), blocked(whole[d, 1, rows, :])
            u, v = blocked(frac[d, 0, rows, :]), blocked(frac[d, 1, rows, :])
            here = 2 * d + band
            T[here, 0] = (a + lane_row + MARGIN).astype(F32)
            T[here, 1] = (b + lane_col + MARGIN).astype(F32)
            for i, w in enumerate(((1.0 - u) * (1.0 - v), (1.0 - u) * v, u * (1.0 - v), u * v)):
                T[here, 2 + i] = w.astype(BF).astype(F32)

    for s, (dy, dx) in enumerate(DIRS):
        @pl.when(has(-dy, -dx))
        def _():
            for f in range(2):
                halo(s, f).wait_recv()

    def shift(i, _):
        for f in range(2):
            F4[f, i, 0 : width + EDGE, :] = F[f, i, :, :][EDGE - MARGIN : EDGE - MARGIN + width + EDGE]
        return 0

    lax.fori_loop(0, height + 2 * MARGIN, shift, 0)

    sub = lax.broadcasted_iota(jnp.int32, (16, 128), 0).astype(F32)

    def warp(q, _):
        for d in range(2):
            for band in range(2):
                here = 2 * d + band
                ry, cx, w00, w01, w10, w11 = (
                    jnp.broadcast_to(T[here, i, pl.ds(q, 1), :], (16, 128)) for i in range(6)
                )
                first, second = sub == cx, sub == cx + 1.0
                upper = jnp.where(first, w00, jnp.where(second, w01, 0.0))
                lower = jnp.where(first, w10, jnp.where(second, w11, 0.0))
                levels = [
                    jnp.where(ry == float(y), upper, jnp.where(ry == float(y - 1), lower, 0.0)).astype(BF)
                    for y in range(16)
                ]
                matrix = jnp.concatenate(levels, axis=0).T
                near = F4[1 - d, pl.ds(band * 8, 16), pl.ds(pl.multiple_of(q * 16, 16), 32), :]
                blocks = []
                for k in range(2):
                    window = near[:, 8 * k : 8 * k + 16].reshape(256, -1)
                    made = jnp.dot(matrix[64 * k : 64 * k + 64], window, preferred_element_type=F32)
                    blocks.append(made.reshape(8, 8, -1))
                Wp[d, pl.ds(1 + band * 8, 8), pl.ds(pl.multiple_of(EDGE + q * 16, 16), 16), :] = (
                    jnp.concatenate(blocks, axis=1).astype(BF)
                )
        return 0

    lax.fori_loop(0, width // 16, warp, 0)

    def border(s):
        dy, dx = DIRS[s]
        return pltpu.make_async_remote_copy(
            src_ref=Wp.at[:, rim(dy, 1, height, 1), rim(dx, EDGE, width, EDGE)],
            dst_ref=Wp.at[:, part(-dy, 1, height, 1), part(-dx, EDGE, width, EDGE)],
            send_sem=rim_send.at[s],
            recv_sem=rim_recv.at[s],
            device_id=at(dy, dx),
            device_id_type=MESH,
        )

    for s, (dy, dx) in enumerate(DIRS):
        @pl.when(has(dy, dx))
        def _():
            border(s).start()

    def push_wait(k, _):
        push(k).wait_recv()
        return 0

    lax.fori_loop(1, n, push_wait, 0)
    every = G[...].reshape(n * 2 * cells, -1)
    source = lax.broadcasted_iota(jnp.int32, (2 * cells, n * 2 * cells), 1)
    warped = jnp.zeros((2 * cells, F.shape[3]), F32)
    for e in range(2):
        chosen = jnp.where(source == index[:, e : e + 1], weight[:, e : e + 1], 0.0).astype(BF)
        warped = warped + jnp.dot(chosen, every, preferred_element_type=F32)
    CW[8] = warped.astype(BF)

    def cell_copy(s):
        dy, dx = DIRS[s]
        return pltpu.make_async_remote_copy(
            src_ref=CW.at[8],
            dst_ref=CW.at[s],
            send_sem=cell_send.at[s],
            recv_sem=cell_recv.at[s],
            device_id=at(dy, dx),
            device_id_type=MESH,
        )

    for s, (dy, dx) in enumerate(DIRS):
        @pl.when(has(dy, dx))
        def _():
            cell_copy(s).start()

        @pl.when(jnp.logical_not(has(-dy, -dx)))
        def _():
            CW[s] = jnp.zeros(CW.shape[1:], BF)

    for s, (dy, dx) in enumerate(DIRS):
        @pl.when(has(-dy, -dx))
        def _():
            border(s).wait_recv()
            cell_copy(s).wait_recv()

    def head(summed):
        hidden = jnp.maximum(summed + conv_b[...], 0.0).astype(BF)
        mixed = jnp.dot(hidden, mix_w[...], preferred_element_type=F32) + mix_b[...]
        return jnp.maximum(mixed, 0.0).astype(BF)

    summed = jnp.zeros((2 * cells, F.shape[3]), F32)
    for dy in (-1, 0, 1):
        own, other = {}, {}
        for dx in (-1, 0, 1):
            oy, ox = at(dy, dx)
            there = has(dy, dx)
            own[dx] = jnp.where(there, G[oy * n_tx + ox].astype(F32), 0.0)
            slot = 8 if dy == 0 and dx == 0 else DIRS.index((-dy, -dx))
            other[dx] = CW[slot].astype(F32)
        columns = []
        for dx in (-1, 0, 1):
            for block in (own, other):
                sides = []
                for d in range(2):
                    lo = d * cells
                    mid = block[0][lo : lo + cells]
                    if dx < 0:
                        mid = jnp.concatenate([block[-1][lo + cells - 1 : lo + cells], mid[: cells - 1]], axis=0)
                    if dx > 0:
                        mid = jnp.concatenate([mid[1:], block[1][lo : lo + 1]], axis=0)
                    sides.append(mid)
                columns.append(jnp.concatenate(sides, axis=0).astype(BF))
        summed = summed + jnp.dot(
            jnp.concatenate(columns, axis=1), conv_w[dy + 1], preferred_element_type=F32
        )
    coarse = head(summed).astype(F32)
    ups = []
    for d in range(2):
        mine = coarse[d * cells : (d + 1) * cells]
        spread = jnp.broadcast_to(mine[:, None, :], (cells, POOL, mine.shape[1])).reshape(width, -1)
        ups.append(nt(out_w[...], spread.astype(BF)) + out_b[...])

    group = 4
    feat = F.shape[3]
    for d in range(2):
        def shifted(i, _):
            rows = (F[d, MARGIN - 1 + i], Wp[d, i])
            for k in range(2):
                for dx in range(3):
                    X[i, :, (2 * dx + k) * feat : (2 * dx + k + 1) * feat] = rows[k][
                        EDGE - 1 + dx : EDGE - 1 + dx + width
                    ]
            return 0

        lax.fori_loop(0, height + 2, shifted, 0)

        def conv(g, _):
            summed = jnp.zeros((group * width, feat), F32)
            for dy in range(3):
                block = X[pl.ds(g * group + dy, group)].reshape(group * width, 6 * feat)
                summed = summed + jnp.dot(block, conv_w[dy], preferred_element_type=F32)
            flow = nt(out_w[...], head(summed)) + out_b[...]
            for j in range(group):
                part_flow = flow[:, j * width : (j + 1) * width] + ups[d]
                for k in range(2):
                    out[d, k, pl.ds(g * group + j, 1), :] = part_flow[k : k + 1]
            return 0

        lax.fori_loop(0, height // group, conv, 0)

    for s, (dy, dx) in enumerate(DIRS):
        @pl.when(has(dy, dx))
        def _():
            for f in range(2):
                halo(s, f).wait_send()
            border(s).wait_send()
            cell_copy(s).wait_send()

    def push_done(k, _):
        push(k).wait_send()
        return 0

    lax.fori_loop(1, n, push_done, 0)


def on_device(
    n_ty, n_tx, frame_zero, frame_one, offset_whole, offset_frac, list_tile, list_pixel, list_weight,
    conv_weight, conv_bias, mix_weight, mix_bias, out_weight, out_bias,
):
    height, width, feat = frame_zero.shape
    cells = width // POOL
    n = n_ty * n_tx
    other = jnp.array([1, 0], jnp.int32).reshape(2, 1, 1, 1)
    index = list_tile * (2 * cells) + other * cells + list_pixel
    index = index.reshape(2, 2, cells).transpose(0, 2, 1).reshape(2 * cells, 2)
    weight = list_weight.reshape(2, 2, cells).transpose(0, 2, 1).reshape(2 * cells, 2).astype(F32)
    out_w = jnp.pad(out_weight.T, ((0, 6), (0, 0)))
    out_b = jnp.pad(out_bias.reshape(2, 1), ((0, 6), (0, 0)))
    vmem = pl.BlockSpec(memory_space=pltpu.VMEM)
    hbm = pl.BlockSpec(memory_space=pl.ANY)
    dma = pltpu.SemaphoreType.DMA
    return pl.pallas_call(
        functools.partial(kernel, n_ty, n_tx, height, width),
        out_shape=jax.ShapeDtypeStruct(offset_frac.shape, F32),
        in_specs=[hbm, hbm] + [vmem] * 10,
        out_specs=vmem,
        scratch_shapes=[
            pltpu.VMEM((2, height + 2 * MARGIN, width + 2 * EDGE, feat), BF),
            pltpu.VMEM((2, height + 2 * MARGIN, width + 2 * EDGE, feat), BF),
            pltpu.VMEM((2, height + 2, width + 2 * EDGE, feat), BF),
            pltpu.VMEM((height + 2, width, 6 * feat), BF),
            pltpu.VMEM((n, 2 * cells, feat), BF),
            pltpu.VMEM((9, 2 * cells, feat), BF),
            pltpu.VMEM((4, 6, 8, 128), F32),
            dma((2,)), dma((8, 2)), dma((8, 2)), dma((n,)), dma((n,)),
            dma((8,)), dma((8,)), dma((8,)), dma((8,)),
        ],
        compiler_params=pltpu.CompilerParams(
            collective_id=0, has_side_effects=True, vmem_limit_bytes=40 * 2**20
        ),
    )(
        frame_zero, frame_one, offset_whole, offset_frac, index, weight,
        conv_weight.reshape(3, 6 * feat, feat), conv_bias.reshape(1, -1), mix_weight,
        mix_bias.reshape(1, -1), out_w, out_b,
    )


def solution(mesh):
    tiles = P(None, None, "ty", "tx")
    in_specs = (P("ty", "tx", None),) * 2 + (tiles,) * 5 + (P(),) * 6
    run = functools.partial(on_device, mesh.shape["ty"], mesh.shape["tx"])
    return jax.shard_map(run, mesh=mesh, in_specs=in_specs, out_specs=tiles, check_vma=False)
```

time: 199 us -> 47.9 us (0.24); the launches traced: 195 us -> 47.4 us
  local copies, waits for them, and re-layouts: 69.3 us -> 8.18 us
  blocking collectives: 43.6 us -> 0 us
  Pallas kernels: 0 us -> 37 us
  starting transfers between devices: 30.8 us -> 0 us
  matrix products: 21.2 us -> 0 us
  other arithmetic: 18.2 us -> 2.18 us
  between operations: 8.32 us -> 0.02 us
  waiting for transfers between devices: 3.84 us -> 0 us
    gather x8 -> x0, local copies, waits for them, and re-layouts: 61.9 us -> none  [on_device(): picked = jnp.take(flat_source, target, axis=0)]
    all_gather x1 -> x0, blocking collectives: 43.6 us -> none  [on_device(): lax.all_gather(coarse.reshape(1, 2, cell_count, channels), ('ty', 'tx'),...]
    pallas_call x0 -> x1, Pallas kernels: none -> 37 us  [on_device(): pl.pallas_call(functools.partial(kernel, n_ty, n_tx, height, width), out_...]
    ppermute x12 -> x0, starting transfers between devices: 30.8 us -> none  [the longest x6 23.1 us: padded_2(): before = lax.ppermute(last, axis, up)]
    dot_general x44 -> x0, matrix products: 21.2 us -> none  [the longest x32 11 us: estimate(): jnp.dot(padded[shift_down:shift_down + tile_height, shift_right:shift_rig...]
    convert_element_type x5 -> x1, other arithmetic: 8.67 us -> 0.68 us  [on_device(): list_weight.reshape(2, 2, cells).transpose(0, 2, 1).reshape(2 * cells, 2)]
    unnamed x68 -> x19, local copies, waits for them, and re-layouts: 0.7 us -> 6.6 us
    ppermute x12 -> x0, waiting for transfers between devices: 3.84 us -> none  [the longest x6 2.29 us: padded_2(): before = lax.ppermute(last, axis, up)]
  transfers between devices with their start and end apart: 12 -> 0, of which waited for: 3 -> 0; matrix products, arithmetic and copies ran while one was open for 7% -> 0% of each run, Pallas kernels for 0% -> 0%
where the time goes in v1:
time: 47.9 us; the launch traced here: 47.4 us
  Pallas kernels  37 us (77%)
  local copies, waits for them, and re-layouts  8.18 us (17%)
  other arithmetic  2.18 us (5%)
    pallas_call x1, Pallas kernels, on_device(): pl.pallas_call(functools.partial(kernel, n_ty, n_tx, height, width), out_...  37 us
    unnamed x19, local copies, waits for them, and re-layouts  6.6 us
    add x2, other arithmetic, on_device(): index = list_tile * (2 * cells) + other * cells + list_pixel  1.5 us

profile of v1, /device:TPU:0, one launch (start us, length us, event | category | flops | bytes accessed | tf_op | source)
XLA Modules:
  0.0 47.4 jit_solution(17346473617507524097)
XLA Ops:
  0.0 0.0 copy-start.8
  0.0 0.0 copy-start.3
  0.0 0.7 %copy-done.8 = s32[2]{0:T(128)S(1)} copy-done((s32[2]{0:T(128)S(1)}, s32[2]{0:T(128)}, u32[]{:S(2)}) %copy-start.8) | copy-done | bytes 32
  0.7 0.7 %multiply_add_fusion = s32[2,2,1,1]{1,3,2,0:T(1,128)S(1)} fusion(s32[2,2,1,1]{1,3,2,0:T(1,128)} %param.18, s32[2]{0:T(128)S(1)} %copy-done.8), kind=kLoop, calls=%fused_computation.2 | loop fusion | flops 8 | bytes 40 | tf_op jit(solution)/shard_map/add | solution.py:344
  1.4 0.8 %broadcast_add_fusion = s32[2,2,1,8]{3,2,1,0:T(1,128)S(1)} fusion(s32[2,2,1,8]{3,2,1,0:T(1,128)} %param.19, s32[2,2]{1,0:T(2,128)S(1)} %bitcast.22), kind=kLoop, calls=%fused_computation.1 | loop fusion | flops 32 | bytes 272 | tf_op jit(solution)/shard_map/add | solution.py:344
  2.2 0.7 %copy.17 = f32[2,1]{1,0:T(2,128)S(1)} copy(f32[2,1]{0,1:T(1,128)} %bitcast.24) | data formatting | bytes 16 | tf_op jit(solution)/shard_map/reshape | solution.py:348
  2.9 0.7 %convert_bitcast_fusion = f32[2,8,2]{1,2,0:T(2,128)S(1)} fusion(bf16[2,2,1,8]{3,1,2,0:T(2,128)(2,1)} %param.20), kind=kLoop, calls=%fused_computation | loop fusion | flops 32 | bytes 192 | tf_op jit(solution)/shard_map/convert_element_type | solution.py:346
  3.6 0.7 %pad.8.out_w = bf16[8,128]{1,0:T(8,128)(2,1)S(1)} pad(bf16[2,128]{1,0:T(2,128)(2,1)} %bitcast.23, bf16[]{:T(256)} %constant.9.clone.1), padding=0_6x0_0 | pad | bytes 2562 | tf_op jit(solution)/shard_map/jit(_pad)/pad | solution.py:347
  4.2 0.1 copy.21
  4.3 0.1 copy.20
  4.4 0.0 copy-start.6
  4.4 0.0 copy-start.7
  4.4 0.0 copy-done.3
  4.4 0.6 %copy-done.6 = f32[128]{0:T(128)S(1)} copy-done((f32[128]{0:T(128)S(1)}, f32[128]{0:T(128)}, u32[]{:S(2)}) %copy-start.6) | copy-done | bytes 536
  5.1 0.0 copy-done.7
  5.1 0.0 copy-start
  5.1 1.1 %copy-done = bf16[9,256,128]{2,1,0:T(8,128)(2,1)S(1)} copy-done((bf16[9,256,128]{2,1,0:T(8,128)(2,1)S(1)}, bf16[9,256,128]{2,1,0:T(8,128)(2,1)}, u32[]{:S(2)}) %copy-start) | copy-done | bytes 589848
  6.2 0.0 copy-start.1
  6.2 1.0 %copy-done.1 = bf16[16,128,128]{2,1,0:T(8,128)(2,1)S(1)} copy-done((bf16[16,128,128]{2,1,0:T(8,128)(2,1)S(1)}, bf16[16,128,128]{2,1,0:T(8,128)(2,1)}, u32[]{:S(2)}) %copy-start.1) | copy-done | bytes 524312
  7.2 1.0 %copy-done.2 = bf16[16,128,128]{2,1,0:T(8,128)(2,1)S(1)} copy-done((bf16[16,128,128]{2,1,0:T(8,128)(2,1)S(1)}, bf16[16,128,128]{2,1,0:T(8,128)(2,1)}, u32[]{:S(2)}) %copy-start.2) | copy-done | bytes 524312
  8.2 0.8 %copy-done.4 = f32[2,2,16,128]{3,2,1,0:T(8,128)S(1)} copy-done((f32[2,2,16,128]{3,2,1,0:T(8,128)S(1)}, f32[2,2,16,128]{3,2,1,0:T(8,128)}, u32[]{:S(2)}) %copy-start.4) | copy-done | bytes 32792
  9.0 0.8 %copy-done.5 = bf16[128,128]{1,0:T(8,128)(2,1)S(1)} copy-done((bf16[128,128]{1,0:T(8,128)(2,1)S(1)}, bf16[128,128]{1,0:T(8,128)(2,1)}, u32[]{:S(2)}) %copy-start.5) | copy-done | bytes 32792
  9.8 37.0 %shard_map.136 = f32[2,2,16,128]{3,2,1,0:T(8,128)S(1)} custom-call(bf16[16,128,128]{2,1,0:T(8,128)(2,1)S(1)} %copy-done.1, bf16[16,128,128]{2,1,0:T(8,128)(2,1)S(1)} %copy-done.2, s32[2,2,16,128]{3,2,1,0:T(8,128)S(1)} %copy-done.3, f32[2,2,16,128]{3,2,1,0:T(8,128)S(1)} %copy-done.4, s32[16,2]{1,0:T(8,128)S(1)} %bitcast.18, f32[16,2]{1,0:T(8,128)S(1)} %bitcast.17, ...), custom_call_target="tpu_custom_call" | custom-call | tf_op jit(solution)/shard_map/pallas_call | solution.py:352
  46.7 0.6 %copy.25 = f32[2,2,16,128]{3,2,1,0:T(8,128)} copy(f32[2,2,16,128]{3,2,1,0:T(8,128)S(1)} %shard_map.136) | data formatting | bytes 65536
  (4 shorter events, 0.0 us)
Async XLA Ops:
  0.0 0.7 %copy-start.8 = (s32[2]{0:T(128)S(1)}, s32[2]{0:T(128)}, u32[]{:S(2)}) copy-start(s32[2]{0:T(128)} %constant.19) | copy-start | bytes 28
  0.0 4.4 %copy-start.3 = (s32[2,2,16,128]{3,2,1,0:T(8,128)S(1)}, s32[2,2,16,128]{3,2,1,0:T(8,128)}, u32[]{:S(2)}) copy-start(s32[2,2,16,128]{3,2,1,0:T(8,128)} %whole.1) | copy-start | bytes 98308
  4.4 0.7 %copy-start.6 = (f32[128]{0:T(128)S(1)}, f32[128]{0:T(128)}, u32[]{:S(2)}) copy-start(f32[128]{0:T(128)} %param.22) | copy-start | bytes 1540
  4.4 0.7 %copy-start.7 = (f32[128]{0:T(128)S(1)}, f32[128]{0:T(128)}, u32[]{:S(2)}) copy-start(f32[128]{0:T(128)} %param.24) | copy-start | bytes 1540
  5.1 1.1 %copy-start = (bf16[9,256,128]{2,1,0:T(8,128)(2,1)S(1)}, bf16[9,256,128]{2,1,0:T(8,128)(2,1)}, u32[]{:S(2)}) copy-start(bf16[9,256,128]{2,1,0:T(8,128)(2,1)} %param.21) | copy-start | bytes 1769476
  6.2 1.0 %copy-start.1 = (bf16[16,128,128]{2,1,0:T(8,128)(2,1)S(1)}, bf16[16,128,128]{2,1,0:T(8,128)(2,1)}, u32[]{:S(2)}) copy-start(bf16[16,128,128]{2,1,0:T(8,128)(2,1)} %f0.1) | copy-start | bytes 1572868
  7.2 1.0 %copy-start.2 = (bf16[16,128,128]{2,1,0:T(8,128)(2,1)S(1)}, bf16[16,128,128]{2,1,0:T(8,128)(2,1)}, u32[]{:S(2)}) copy-start(bf16[16,128,128]{2,1,0:T(8,128)(2,1)} %f1.1) | copy-start | bytes 1572868
  8.2 0.8 %copy-start.4 = (f32[2,2,16,128]{3,2,1,0:T(8,128)S(1)}, f32[2,2,16,128]{3,2,1,0:T(8,128)}, u32[]{:S(2)}) copy-start(f32[2,2,16,128]{3,2,1,0:T(8,128)} %frac.1) | copy-start | bytes 98308
  9.0 0.8 %copy-start.5 = (bf16[128,128]{1,0:T(8,128)(2,1)S(1)}, bf16[128,128]{1,0:T(8,128)(2,1)}, u32[]{:S(2)}) copy-start(bf16[128,128]{1,0:T(8,128)(2,1)} %mix_w.1) | copy-start | bytes 98308

commit v2 on v1

v2 whole, which is shorter than its diff:
```python
import functools

import jax
import jax.numpy as jnp
from jax import lax
from jax.experimental import pallas as pl
from jax.experimental.pallas import tpu as pltpu
from jax.sharding import PartitionSpec as P

POOL = 16
MARGIN = 4
EDGE = 16
DIRS = [(-1, 0), (1, 0), (0, -1), (0, 1), (-1, -1), (-1, 1), (1, -1), (1, 1)]
MESH = pl.DeviceIdType.MESH
BF = jnp.bfloat16
F32 = jnp.float32


def part(step, center, size, margin):
    if step < 0:
        return pl.ds(center - margin, margin)
    if step > 0:
        return pl.ds(center + size, margin)
    return pl.ds(center, size)


def rim(step, start, size, margin):
    if step < 0:
        return pl.ds(start, margin)
    if step > 0:
        return pl.ds(start + size - margin, margin)
    return pl.ds(start, size)


def nt(a, b):
    return lax.dot_general(a, b, (((1,), (1,)), ((), ())), preferred_element_type=F32)


def kernel(
    n_ty, n_tx, height, width,
    f0, f1, whole_in, frac_in, tiles, pixel_in, weight_in, conv_in, conv_b_in, mix_in, mix_b_in, out_in, out_b,
    out,
    F, F4, Wp, X, G, CW, T, whole, frac, pixel, weight, W2, mix2, conv_b, mix_b, out_w,
    load_sem, halo_send, halo_recv, all_send, all_recv, rim_send, rim_recv, side_send, side_recv, cell_send, cell_recv,
):
    n = n_ty * n_tx
    ty, tx = lax.axis_index("ty"), lax.axis_index("tx")
    me = ty * n_tx + tx
    frames = (f0, f1)
    cells = width // POOL
    feat = F.shape[3]

    def has(dy, dx):
        return (ty + dy >= 0) & (ty + dy < n_ty) & (tx + dx >= 0) & (tx + dx < n_tx)

    def at(dy, dx):
        return (lax.rem(ty + dy + n_ty, n_ty), lax.rem(tx + dx + n_tx, n_tx))

    barrier = pltpu.get_barrier_semaphore()

    def greet(k, _):
        other = lax.rem(me + k, n)
        pl.semaphore_signal(
            barrier, inc=1, device_id=(other // n_tx, lax.rem(other, n_tx)), device_id_type=MESH
        )
        return 0

    lax.fori_loop(1, n, greet, 0)

    moves = [(frames[f], F.at[f, pl.ds(MARGIN, height), pl.ds(EDGE, width)]) for f in range(2)]
    moves += [(whole_in, whole), (frac_in, frac), (pixel_in, pixel), (weight_in, weight)]
    moves += [
        (conv_in, W2.at[pl.ds(0, 3), :, pl.ds(0, feat)]),
        (conv_in, W2.at[pl.ds(1, 3), :, pl.ds(feat, feat)]),
        (mix_in, mix2.at[pl.ds(0, feat), pl.ds(0, feat)]),
        (mix_in, mix2.at[pl.ds(feat, feat), pl.ds(feat, feat)]),
        (conv_b_in, conv_b), (mix_b_in, mix_b), (out_in, out_w),
    ]
    loads = [pltpu.make_async_copy(src, dst, load_sem.at[i]) for i, (src, dst) in enumerate(moves)]
    for load in loads:
        load.start()

    for dy, dx in DIRS:
        @pl.when(jnp.logical_not(has(dy, dx)))
        def _():
            rows, cols = part(dy, MARGIN, height, MARGIN), part(dx, EDGE, width, EDGE)
            F[:, rows, cols, :] = jnp.zeros((2, rows.size, cols.size, feat), BF)
            rows = part(dy, 1, height, 1)
            Wp[:, rows, cols, :] = jnp.zeros((2, rows.size, cols.size, feat), BF)

    pl.semaphore_wait(barrier, n - 1)

    def halo(s, f):
        dy, dx = DIRS[s]
        return pltpu.make_async_remote_copy(
            src_ref=frames[f].at[rim(dy, 0, height, MARGIN), rim(dx, 0, width, EDGE)],
            dst_ref=F.at[f, part(-dy, MARGIN, height, MARGIN), part(-dx, EDGE, width, EDGE)],
            send_sem=halo_send.at[s, f],
            recv_sem=halo_recv.at[s, f],
            device_id=at(dy, dx),
            device_id_type=MESH,
        )

    for s, (dy, dx) in enumerate(DIRS):
        @pl.when(has(dy, dx))
        def _():
            for f in range(2):
                halo(s, f).start()

    def halo_wait(sides):
        for s in sides:
            dy, dx = DIRS[s]

            @pl.when(has(-dy, -dx))
            def _():
                for f in range(2):
                    halo(s, f).wait_recv()

    for load in loads[:2]:
        load.wait()
    pooled = []
    for f in range(2):
        def add_row(r, total):
            return total + F[f, MARGIN + r, EDGE : EDGE + width, :].astype(F32)

        total = lax.fori_loop(0, height, add_row, jnp.zeros((width, feat), F32))
        pooled.append(jnp.sum(total.reshape(cells, POOL, -1), axis=1) / POOL)
    G[me] = jnp.concatenate(pooled, axis=0).astype(BF)

    def push(k):
        other = lax.rem(me + k, n)
        return pltpu.make_async_remote_copy(
            src_ref=G.at[me],
            dst_ref=G.at[me],
            send_sem=all_send.at[k],
            recv_sem=all_recv.at[k],
            device_id=(other // n_tx, lax.rem(other, n_tx)),
            device_id_type=MESH,
        )

    def push_start(k, _):
        push(k).start()
        return 0

    lax.fori_loop(1, n, push_start, 0)

    for load in loads[2:]:
        load.wait()
    lane = lax.broadcasted_iota(jnp.int32, (8, 128), 1)
    pair = lax.broadcasted_iota(jnp.int32, (8, 128), 0)
    lane_row = (lane // 8) % 8
    lane_col = lane % 8
    source_lane = (2 * pair + lane // 64) * 8 + lane_col

    def blocked(rows):
        got = jnp.zeros((8, 128), rows.dtype)
        for r in range(8):
            row = jnp.broadcast_to(rows[r : r + 1, :], (8, 128))
            picked = jnp.take_along_axis(row, source_lane, axis=1, mode="promise_in_bounds")
            got = jnp.where(lane_row == r, picked, got)
        return got

    for d in range(2):
        for band in range(2):
            rows = pl.ds(band * 8, 8)
            a, b = blocked(whole[d, 0, rows, :]), blocked(whole[d, 1, rows, :])
            u, v = blocked(frac[d, 0, rows, :]), blocked(frac[d, 1, rows, :])
            here = 2 * d + band
            T[here, 0] = (a + lane_row + MARGIN).astype(F32)
            T[here, 1] = (b + lane_col + MARGIN).astype(F32)
            for i, w in enumerate(((1.0 - u) * (1.0 - v), (1.0 - u) * v, u * (1.0 - v), u * v)):
                T[here, 2 + i] = w.astype(BF).astype(F32)

    W2[0, :, feat:] = jnp.zeros((6 * feat, feat), BF)
    W2[3, :, :feat] = jnp.zeros((6 * feat, feat), BF)
    mix2[:feat, feat:] = jnp.zeros((feat, feat), BF)
    mix2[feat:, :feat] = jnp.zeros((feat, feat), BF)
    flat = jnp.concatenate([out_w[...].astype(F32), jnp.zeros((6, feat), F32)], axis=0)
    lower = jnp.concatenate([jnp.zeros((2, feat), F32), flat[:6]], axis=0)
    out_two = jnp.concatenate([flat, lower], axis=1).astype(BF)
    out_one = flat.astype(BF)

    def shift(i):
        for f in range(2):
            F4[f, i, 0 : width + EDGE, :] = F[f, i, :, :][EDGE - MARGIN : EDGE - MARGIN + width + EDGE]

    def spread(k, i):
        for d in range(2):
            row = F[d, MARGIN - 1 + i] if k == 0 else Wp[d, i]
            for dx in range(3):
                X[d, i, :, (2 * dx + k) * feat : (2 * dx + k + 1) * feat] = row[
                    EDGE - 1 + dx : EDGE - 1 + dx + width
                ]

    def loop(count, start, step):
        def once(i, _):
            step(start + i)
            return 0

        lax.fori_loop(0, count, once, 0)

    sub = lax.broadcasted_iota(jnp.int32, (16, 128), 0).astype(F32)

    def warp_pair(band, d, q):
        here = 2 * d + band
        ry, cx, w00, w01, w10, w11 = (
            jnp.broadcast_to(T[here, i, pl.ds(q, 1), :], (16, 128)) for i in range(6)
        )
        first, second = sub == cx, sub == cx + 1.0
        upper = jnp.where(first, w00, jnp.where(second, w01, 0.0))
        lower = jnp.where(first, w10, jnp.where(second, w11, 0.0))
        levels = [
            jnp.where(ry == float(y), upper, jnp.where(ry == float(y - 1), lower, 0.0)).astype(BF)
            for y in range(16)
        ]
        matrix = jnp.concatenate(levels, axis=0).T
        near = F4[1 - d, pl.ds(band * 8, 16), pl.ds(pl.multiple_of(q * 16, 16), 32), :]
        blocks = []
        for k in range(2):
            window = near[:, 8 * k : 8 * k + 16].reshape(256, -1)
            made = jnp.dot(matrix[64 * k : 64 * k + 64], window, preferred_element_type=F32)
            blocks.append(made.reshape(8, 8, -1))
        Wp[d, pl.ds(1 + band * 8, 8), pl.ds(pl.multiple_of(EDGE + q * 16, 16), 16), :] = (
            jnp.concatenate(blocks, axis=1).astype(BF)
        )

    def warp(band):
        def two(i):
            for q in range(2):
                for d in range(2):
                    warp_pair(band, d, 2 * i + q)

        loop(width // 32, 0, two)

    def side(s, band, turn):
        dy, dx = DIRS[s]
        rows = pl.ds(1 + 8 * band, 8)
        return pltpu.make_async_remote_copy(
            src_ref=Wp.at[:, rows, rim(dx, EDGE, width, EDGE)],
            dst_ref=Wp.at[:, rows, part(-dx, EDGE, width, EDGE)],
            send_sem=side_send.at[s, turn],
            recv_sem=side_recv.at[s, turn],
            device_id=at(dy, dx),
            device_id_type=MESH,
        )

    def border(s):
        dy, dx = DIRS[s]
        return pltpu.make_async_remote_copy(
            src_ref=Wp.at[:, rim(dy, 1, height, 1), rim(dx, EDGE, width, EDGE)],
            dst_ref=Wp.at[:, part(-dy, 1, height, 1), part(-dx, EDGE, width, EDGE)],
            send_sem=rim_send.at[s],
            recv_sem=rim_recv.at[s],
            device_id=at(dy, dx),
            device_id_type=MESH,
        )

    def cell_copy(s):
        dy, dx = DIRS[s]
        return pltpu.make_async_remote_copy(
            src_ref=CW.at[8],
            dst_ref=CW.at[s],
            send_sem=cell_send.at[s],
            recv_sem=cell_recv.at[s],
            device_id=at(dy, dx),
            device_id_type=MESH,
        )

    def each(sides, sign, act):
        for s in sides:
            dy, dx = DIRS[s]

            @pl.when(has(sign * dy, sign * dx))
            def _():
                act(s)

    across = (2, 3)
    along = (0, 1, 4, 5, 6, 7)
    everywhere = range(8)

    def coarse_warp():
        def push_wait(k, _):
            push(k).wait_recv()
            return 0

        lax.fori_loop(1, n, push_wait, 0)
        every = G[...].reshape(n * 2 * cells, -1)
        source = lax.broadcasted_iota(jnp.int32, (2 * cells, n * 2 * cells), 1).astype(F32)
        small = lax.broadcasted_iota(jnp.int32, (cells, cells), 0) == lax.broadcasted_iota(
            jnp.int32, (cells, cells), 1
        )
        warped = jnp.zeros((2 * cells, feat), F32)
        for e in range(2):
            names, shares = [], []
            for d in range(2):
                base = tiles[d, 0, 0, e] * (2 * cells) + (1 - d) * cells
                row = (pixel[d, e] + base).astype(F32)
                names.append(jnp.sum(jnp.where(small, row, 0.0), axis=1, keepdims=True))
                row = weight[d, 0][e : e + 1].astype(F32)
                shares.append(jnp.sum(jnp.where(small, row, 0.0), axis=1, keepdims=True))
            names, shares = jnp.concatenate(names, axis=0), jnp.concatenate(shares, axis=0)
            chosen = jnp.where(source == names, shares, 0.0).astype(BF)
            warped = warped + jnp.dot(chosen, every, preferred_element_type=F32)
        CW[8] = warped.astype(BF)
        for s, (dy, dx) in enumerate(DIRS):
            @pl.when(jnp.logical_not(has(-dy, -dx)))
            def _():
                CW[s] = jnp.zeros(CW.shape[1:], BF)

        each(everywhere, 1, lambda s: cell_copy(s).start())

    def coarse_flow():
        each(everywhere, -1, lambda s: cell_copy(s).wait_recv())
        summed = jnp.zeros((2 * cells, feat), F32)
        for dy in (-1, 0, 1):
            own, other = {}, {}
            for dx in (-1, 0, 1):
                oy, ox = at(dy, dx)
                there = has(dy, dx)
                own[dx] = jnp.where(there, G[oy * n_tx + ox].astype(F32), 0.0)
                slot = 8 if dy == 0 and dx == 0 else DIRS.index((-dy, -dx))
                other[dx] = CW[slot].astype(F32)
            columns = []
            for dx in (-1, 0, 1):
                for block in (own, other):
                    sides = []
                    for d in range(2):
                        lo = d * cells
                        mid = block[0][lo : lo + cells]
                        if dx < 0:
                            mid = jnp.concatenate([block[-1][lo + cells - 1 : lo + cells], mid[: cells - 1]], axis=0)
                        if dx > 0:
                            mid = jnp.concatenate([mid[1:], block[1][lo : lo + 1]], axis=0)
                        sides.append(mid)
                    columns.append(jnp.concatenate(sides, axis=0).astype(BF))
            summed = summed + jnp.dot(
                jnp.concatenate(columns, axis=1), W2[dy + 1, :, :feat], preferred_element_type=F32
            )
        hidden = jnp.maximum(summed + conv_b[...], 0.0).astype(BF)
        mixed = jnp.dot(hidden, mix2[:feat, :feat], preferred_element_type=F32) + mix_b[...]
        coarse = jnp.maximum(mixed, 0.0)
        ups = []
        for d in range(2):
            mine = coarse[d * cells : (d + 1) * cells]
            wide = jnp.broadcast_to(mine[:, None, :], (cells, POOL, feat)).reshape(width, -1)
            ups.append(nt(out_one, wide.astype(BF)))
        return ups

    conv_b2 = jnp.concatenate([conv_b[...]] * 2, axis=1)
    mix_b2 = jnp.concatenate([mix_b[...]] * 2, axis=1)

    def conv(start, pairs):
        def one(d):
            lhs = jnp.concatenate(
                [
                    jnp.concatenate([X[d, start + 2 * p + s] for p in range(pairs)], axis=0)
                    for s in range(4)
                ],
                axis=1,
            )
            summed = jnp.dot(lhs, W2[...].reshape(4 * 6 * feat, 2 * feat), preferred_element_type=F32)
            hidden = jnp.maximum(summed + conv_b2, 0.0).astype(BF)
            mixed = jnp.dot(hidden, mix2[...], preferred_element_type=F32) + mix_b2
            flow = nt(out_two, jnp.maximum(mixed, 0.0).astype(BF))
            for p in range(pairs):
                for j in range(2):
                    for k in range(2):
                        out[d, k, pl.ds(start + 2 * p + j, 1), :] = (
                            flow[2 * j + k : 2 * j + k + 1, p * width : (p + 1) * width] + out_b[k]
                        )

        loop(2, 0, one)

    if n_ty == 2:
        one = ty
        two = 1 - ty
        halo_wait(across)
        loop(height + MARGIN, MARGIN * one, shift)
        loop(height + 1, one, functools.partial(spread, 0))
        warp(one)
        each(across, 1, lambda s: side(s, one, 0).start())
        coarse_warp()
        each(across, -1, lambda s: side(s, one, 0).wait_recv())
        loop(9, 9 * one, functools.partial(spread, 1))
        conv(10 * one, 3)
        halo_wait(along)
        loop(MARGIN, (height + MARGIN) * two, shift)
        spread(0, (height + 1) * two)
        warp(two)
        each(along, 1, lambda s: border(s).start())
        each(across, 1, lambda s: side(s, two, 1).start())
        ups = coarse_flow()
        each(across, -1, lambda s: side(s, two, 1).wait_recv())
        loop(8, 1 + 8 * two, functools.partial(spread, 1))
        conv(2 + 4 * two, 4)
        each(along, -1, lambda s: border(s).wait_recv())
        spread(1, (height + 1) * two)
        conv(14 * two, 1)
    else:
        one, two = 0, 1
        halo_wait(everywhere)
        loop(height + 2 * MARGIN, 0, shift)
        loop(height + 2, 0, functools.partial(spread, 0))
        warp(0)
        warp(1)
        each(along, 1, lambda s: border(s).start())
        each(across, 1, lambda s: side(s, 0, 0).start())
        each(across, 1, lambda s: side(s, 1, 1).start())
        coarse_warp()
        ups = coarse_flow()
        each(along, -1, lambda s: border(s).wait_recv())
        each(across, -1, lambda s: side(s, 0, 0).wait_recv())
        each(across, -1, lambda s: side(s, 1, 1).wait_recv())
        loop(height + 2, 0, functools.partial(spread, 1))
        conv(0, 4)
        conv(8, 4)

    for d in range(2):
        for k in range(2):
            out[d, k] = out[d, k] + (ups[d][k : k + 1] + out_b[k])

    for f in range(2):
        each(everywhere, 1, lambda s: halo(s, f).wait_send())
    each(along, 1, lambda s: border(s).wait_send())
    each(across, 1, lambda s: side(s, one, 0).wait_send())
    each(across, 1, lambda s: side(s, two, 1).wait_send())
    each(everywhere, 1, lambda s: cell_copy(s).wait_send())

    def push_done(k, _):
        push(k).wait_send()
        return 0

    lax.fori_loop(1, n, push_done, 0)


def on_device(
    n_ty, n_tx, frame_zero, frame_one, offset_whole, offset_frac, list_tile, list_pixel, list_weight,
    conv_weight, conv_bias, mix_weight, mix_bias, out_weight, out_bias,
):
    height, width, feat = frame_zero.shape
    cells = width // POOL
    n = n_ty * n_tx
    vmem = pl.BlockSpec(memory_space=pltpu.VMEM)
    smem = pl.BlockSpec(memory_space=pltpu.SMEM)
    hbm = pl.BlockSpec(memory_space=pl.ANY)
    dma = pltpu.SemaphoreType.DMA
    return pl.pallas_call(
        functools.partial(kernel, n_ty, n_tx, height, width),
        out_shape=jax.ShapeDtypeStruct(offset_frac.shape, F32),
        in_specs=[hbm] * 4 + [smem] + [hbm] * 7 + [smem],
        out_specs=vmem,
        scratch_shapes=[
            pltpu.VMEM((2, height + 2 * MARGIN, width + 2 * EDGE, feat), BF),
            pltpu.VMEM((2, height + 2 * MARGIN, width + EDGE, feat), BF),
            pltpu.VMEM((2, height + 2, width + 2 * EDGE, feat), BF),
            pltpu.VMEM((2, height + 2, width, 6 * feat), BF),
            pltpu.VMEM((n, 2 * cells, feat), BF),
            pltpu.VMEM((9, 2 * cells, feat), BF),
            pltpu.VMEM((4, 6, 8, 128), F32),
            pltpu.VMEM(offset_whole.shape, jnp.int32),
            pltpu.VMEM(offset_frac.shape, F32),
            pltpu.VMEM(list_pixel.shape, jnp.int32),
            pltpu.VMEM((2, 1, 2, cells), BF),
            pltpu.VMEM((4, 6 * feat, 2 * feat), BF),
            pltpu.VMEM((2 * feat, 2 * feat), BF),
            pltpu.VMEM((1, feat), F32),
            pltpu.VMEM((1, feat), F32),
            pltpu.VMEM((2, feat), BF),
            dma((13,)), dma((8, 2)), dma((8, 2)), dma((n,)), dma((n,)),
            dma((8,)), dma((8,)), dma((8, 2)), dma((8, 2)), dma((8,)), dma((8,)),
        ],
        compiler_params=pltpu.CompilerParams(
            collective_id=0, has_side_effects=True, vmem_limit_bytes=60 * 2**20
        ),
    )(
        frame_zero, frame_one, offset_whole, offset_frac, list_tile.transpose(0, 2, 3, 1), list_pixel,
        list_weight.transpose(0, 2, 1, 3), conv_weight.reshape(3, 6 * feat, feat), conv_bias.reshape(1, -1), mix_weight,
        mix_bias.reshape(1, -1), out_weight.T, out_bias,
    )


def solution(mesh):
    tiles = P(None, None, "ty", "tx")
    in_specs = (P("ty", "tx", None),) * 2 + (tiles,) * 5 + (P(),) * 6
    run = functools.partial(on_device, mesh.shape["ty"], mesh.shape["tx"])
    return jax.shard_map(run, mesh=mesh, in_specs=in_specs, out_specs=tiles, check_vma=False)
```

time: 47.9 us -> 35.3 us (0.74)
  the two profiles are of different devices: /device:TPU:0 before, /device:TPU:1 now
where the time goes in v2:
time: 35.3 us; the launch traced here: 35.1 us
  Pallas kernels  33.7 us (95%)
  local copies, waits for them, and re-layouts  1.38 us (4%)
    pallas_call x1, Pallas kernels, on_device(): pl.pallas_call(functools.partial(kernel, n_ty, n_tx, height, width), out_...  33.7 us
    unnamed x1, local copies, waits for them, and re-layouts  1.38 us

profile of v2, /device:TPU:1, one launch (start us, length us, event | category | flops | bytes accessed | tf_op | source)
XLA Modules:
  0.0 35.1 jit_solution(16233229096126797155)
XLA Ops:
  0.0 33.7 %shard_map.127 = f32[2,2,16,128]{3,2,1,0:T(8,128)} custom-call(bf16[16,128,128]{2,1,0:T(8,128)(2,1)} %f0.1, bf16[16,128,128]{2,1,0:T(8,128)(2,1)} %f1.1, s32[2,2,16,128]{3,2,1,0:T(8,128)} %whole_in.1, f32[2,2,16,128]{3,2,1,0:T(8,128)} %frac_in.1, s32[2,1,1,2]{3,2,1,0:T(1,128)} %bitcast.11, s32[2,2,1,8]{3,2,1,0:T(1,128)} %pixel_in.1, ...), custom_call_target="tpu_custom_call" | custom-call | tf_op jit(solution)/shard_map/pallas_call | solution.py:447
  33.7 1.4 %copy.17 = f32[2,2,16,128]{3,2,1,0:T(8,128)} copy(f32[2,2,16,128]{3,2,1,0:T(8,128)} %shard_map.127) | data formatting | bytes 65536

commit v3 on v2

--- a/solution.py
+++ b/solution.py
@@ -40,12 +40,20 @@
     n_ty, n_tx, height, width,
     f0, f1, whole_in, frac_in, tiles, pixel_in, weight_in, conv_in, conv_b_in, mix_in, mix_b_in, out_in, out_b,
     out,
-    F, F4, Wp, X, G, CW, T, whole, frac, pixel, weight, W2, mix2, conv_b, mix_b, out_w,
-    load_sem, halo_send, halo_recv, all_send, all_recv, rim_send, rim_recv, side_send, side_recv, cell_send, cell_recv,
+    F, F4, Wp, X, G, CW, T, LB, PO, PI, CI, SO, SI, SC, whole, frac, pixel, weight, W2, mix2, conv_b, mix_b, out_w,
+    load_sem, halo_send, halo_recv, all_send, all_recv, rim_send, rim_recv, side_send, side_recv, list_send, list_recv,
 ):
     n = n_ty * n_tx
     ty, tx = lax.axis_index("ty"), lax.axis_index("tx")
-    me = ty * n_tx + tx
+    tx_bits, ty_bits = n_tx.bit_length() - 1, n_ty.bit_length() - 1
+    assert n_tx == 1 << tx_bits and n_ty == 1 << ty_bits
+    steps = [(1, b) for b in range(tx_bits - 1, 0, -1)] + [(0, b) for b in range(ty_bits - 1, -1, -1)]
+    steps += [(1, 0)] if tx_bits else []
+
+    def slot_of(place):
+        return sum(lax.rem(place[which] // (1 << b), 2) * (1 << j) for j, (which, b) in enumerate(steps))
+
+    me = slot_of((ty, tx))
     frames = (f0, f1)
     cells = width // POOL
     feat = F.shape[3]
@@ -58,14 +66,23 @@
 
     barrier = pltpu.get_barrier_semaphore()
 
-    def greet(k, _):
-        other = lax.rem(me + k, n)
-        pl.semaphore_signal(
-            barrier, inc=1, device_id=(other // n_tx, lax.rem(other, n_tx)), device_id_type=MESH
-        )
-        return 0
-
-    lax.fori_loop(1, n, greet, 0)
+    def mate(step):
+        which, b = step
+        place = [ty, tx]
+        place[which] = place[which] + (1 << b) * (1 - 2 * lax.rem(place[which] // (1 << b), 2))
+        return tuple(place)
+
+    def greet(there):
+        pl.semaphore_signal(barrier, inc=1, device_id=there, device_id_type=MESH)
+
+    for dy, dx in DIRS:
+        @pl.when(has(dy, dx))
+        def _():
+            greet(at(dy, dx))
+
+    far = [step for step in steps if step[1] > 0]
+    for step in far:
+        greet(mate(step))
 
     moves = [(frames[f], F.at[f, pl.ds(MARGIN, height), pl.ds(EDGE, width)]) for f in range(2)]
     moves += [(whole_in, whole), (frac_in, frac), (pixel_in, pixel), (weight_in, weight)]
@@ -88,24 +105,86 @@
             rows = part(dy, 1, height, 1)
             Wp[:, rows, cols, :] = jnp.zeros((2, rows.size, cols.size, feat), BF)
 
-    pl.semaphore_wait(barrier, n - 1)
-
-    def halo(s, f):
+    for load in loads[4:6]:
+        load.wait()
+    LB[8] = jnp.zeros((8, 128), F32)
+    for d in range(2):
+        for e in range(2):
+            tile = tiles[d, 0, 0, e]
+            base = slot_of((tile // n_tx, lax.rem(tile, n_tx))) * (2 * cells) + (1 - d) * cells
+            LB[8, 2 * d + e : 2 * d + e + 1, :cells] = (pixel[d, e] + base).astype(F32)
+            LB[8, 4 + 2 * d + e : 5 + 2 * d + e, :cells] = weight[d, 0].astype(F32)[e : e + 1]
+    for s, (dy, dx) in enumerate(DIRS):
+        @pl.when(jnp.logical_not(has(-dy, -dx)))
+        def _():
+            LB[s] = jnp.zeros((8, 128), F32)
+
+    for load in loads[:2]:
+        load.wait()
+
+    def pack(g, _):
+        for f in range(2):
+            rows = [MARGIN + 4 * g + i for i in range(4)]
+            left = [F[f, row, EDGE : 2 * EDGE, :].astype(F32)[:MARGIN] for row in rows]
+            right = [F[f, row, width : width + EDGE, :].astype(F32)[EDGE - MARGIN :] for row in rows]
+            here = pl.ds(pl.multiple_of(16 * g, 16), 16)
+            PO[0, f, here, :] = jnp.concatenate(left, axis=0).astype(BF)
+            PO[1, f, here, :] = jnp.concatenate(right, axis=0).astype(BF)
+        return 0
+
+    lax.fori_loop(0, height // 4, pack, 0)
+
+    peers = sum(jnp.where(has(dy, dx), 1, 0) for dy, dx in DIRS) + len(far)
+    pl.semaphore_wait(barrier, peers)
+
+    def halo(s):
         dy, dx = DIRS[s]
+        hand = 0 if dx < 0 else 1
+        if dx == 0:
+            src = F.at[:, rim(dy, MARGIN, height, MARGIN), pl.ds(EDGE, width)]
+            dst = F.at[:, part(-dy, MARGIN, height, MARGIN), pl.ds(EDGE, width)]
+        elif dy == 0:
+            src, dst = PO.at[hand], PI.at[hand]
+        else:
+            src, dst = PO.at[hand, :, pl.ds(0 if dy < 0 else 4 * height - 16, 16)], CI.at[s - 4]
         return pltpu.make_async_remote_copy(
-            src_ref=frames[f].at[rim(dy, 0, height, MARGIN), rim(dx, 0, width, EDGE)],
-            dst_ref=F.at[f, part(-dy, MARGIN, height, MARGIN), part(-dx, EDGE, width, EDGE)],
-            send_sem=halo_send.at[s, f],
-            recv_sem=halo_recv.at[s, f],
+            src_ref=src,
+            dst_ref=dst,
+            send_sem=halo_send.at[s],
+            recv_sem=halo_recv.at[s],
             device_id=at(dy, dx),
             device_id_type=MESH,
         )
 
-    for s, (dy, dx) in enumerate(DIRS):
-        @pl.when(has(dy, dx))
+    def list_copy(s):
+        return pltpu.make_async_remote_copy(
+            src_ref=LB.at[8],
+            dst_ref=LB.at[s],
+            send_sem=list_send.at[s],
+            recv_sem=list_recv.at[s],
+            device_id=at(*DIRS[s]),
+            device_id_type=MESH,
+        )
+
+    for s in (2, 3, 4, 5, 6, 7, 0, 1):
+        @pl.when(has(*DIRS[s]))
         def _():
-            for f in range(2):
-                halo(s, f).start()
+            halo(s).start()
+
+    for s in range(8):
+        @pl.when(has(*DIRS[s]))
+        def _():
+            list_copy(s).start()
+
+    def unpack(tile, f, start, hand):
+        tile = tile.astype(F32)
+        rest = jnp.zeros((EDGE - MARGIN, feat), F32)
+        for i in range(4):
+            piece = tile[4 * i : 4 * i + 4]
+            if hand == 0:
+                F[f, start + i, EDGE + width :, :] = jnp.concatenate([piece, rest], axis=0).astype(BF)
+            else:
+                F[f, start + i, :EDGE, :] = jnp.concatenate([rest, piece], axis=0).astype(BF)
 
     def halo_wait(sides):
         for s in sides:
@@ -113,11 +192,19 @@
 
             @pl.when(has(-dy, -dx))
             def _():
+                halo(s).wait_recv()
+                hand = 0 if dx < 0 else 1
                 for f in range(2):
-                    halo(s, f).wait_recv()
-
-    for load in loads[:2]:
-        load.wait()
+                    if dx != 0 and dy == 0:
+                        def group(g, _):
+                            tile = PI[hand, f, pl.ds(pl.multiple_of(16 * g, 16), 16), :]
+                            unpack(tile, f, MARGIN + 4 * g, hand)
+                            return 0
+
+                        lax.fori_loop(0, height // 4, group, 0)
+                    elif dx != 0:
+                        unpack(CI[s - 4, f], f, MARGIN + height if dy < 0 else 0, hand)
+
     pooled = []
     for f in range(2):
         def add_row(r, total):
@@ -127,24 +214,27 @@
         pooled.append(jnp.sum(total.reshape(cells, POOL, -1), axis=1) / POOL)
     G[me] = jnp.concatenate(pooled, axis=0).astype(BF)
 
-    def push(k):
-        other = lax.rem(me + k, n)
+    def hand(j):
+        span = 1 << j
+        held = pl.ds(me - lax.rem(me, span), span)
         return pltpu.make_async_remote_copy(
-            src_ref=G.at[me],
-            dst_ref=G.at[me],
-            send_sem=all_send.at[k],
-            recv_sem=all_recv.at[k],
-            device_id=(other // n_tx, lax.rem(other, n_tx)),
+            src_ref=G.at[held],
+            dst_ref=G.at[held],
+            send_sem=all_send.at[j],
+            recv_sem=all_recv.at[j],
+            device_id=mate(steps[j]),
             device_id_type=MESH,
         )
 
-    def push_start(k, _):
-        push(k).start()
-        return 0
-
-    lax.fori_loop(1, n, push_start, 0)
-
-    for load in loads[2:]:
+    def hand_on(j):
+        if j > 0 and j <= len(steps):
+            hand(j - 1).wait_recv()
+        if j < len(steps):
+            hand(j).start()
+
+    hand_on(0)
+
+    for load in loads[2:4] + loads[6:]:
         load.wait()
     lane = lax.broadcasted_iota(jnp.int32, (8, 128), 1)
     pair = lax.broadcasted_iota(jnp.int32, (8, 128), 0)
@@ -232,39 +322,61 @@
 
         loop(width // 32, 0, two)
 
-    def side(s, band, turn):
-        dy, dx = DIRS[s]
-        rows = pl.ds(1 + 8 * band, 8)
+    def side(s, turn):
         return pltpu.make_async_remote_copy(
-            src_ref=Wp.at[:, rows, rim(dx, EDGE, width, EDGE)],
-            dst_ref=Wp.at[:, rows, part(-dx, EDGE, width, EDGE)],
+            src_ref=SO.at[turn, s - 2],
+            dst_ref=SI.at[turn, s - 2],
             send_sem=side_send.at[s, turn],
             recv_sem=side_recv.at[s, turn],
-            device_id=at(dy, dx),
+            device_id=at(*DIRS[s]),
             device_id_type=MESH,
         )
+
+    def side_pack(band, turn):
+        for hand in range(2):
+            lo, col = (EDGE, 0) if hand == 0 else (width, EDGE - 1)
+            ends = [
+                Wp[d, 1 + 8 * band + i, lo : lo + EDGE, :].astype(F32)[col : col + 1]
+                for d in range(2) for i in range(8)
+            ]
+            SO[turn, hand] = jnp.concatenate(ends, axis=0).astype(BF)
+
+    def side_column(d, row, hand, value):
+        cols = pl.ds(EDGE + width, EDGE) if hand == 0 else pl.ds(0, EDGE)
+        Wp[d, row, cols, :] = jnp.broadcast_to(value, (EDGE, feat)).astype(BF)
+
+    def side_unpack(s, band, turn):
+        side(s, turn).wait_recv()
+        tile = SI[turn, s - 2].astype(F32)
+        for d in range(2):
+            for i in range(8):
+                side_column(d, 1 + 8 * band + i, s - 2, tile[8 * d + i : 8 * d + i + 1])
 
     def border(s):
         dy, dx = DIRS[s]
+        if dx == 0:
+            src = Wp.at[:, rim(dy, 1, height, 1), pl.ds(EDGE, width)]
+            dst = Wp.at[:, part(-dy, 1, height, 1), pl.ds(EDGE, width)]
+        else:
+            turn = 1 if n_ty == 2 or dy > 0 else 0
+            src, dst = SO.at[turn, 0 if dx < 0 else 1], SC.at[s - 4]
         return pltpu.make_async_remote_copy(
-            src_ref=Wp.at[:, rim(dy, 1, height, 1), rim(dx, EDGE, width, EDGE)],
-            dst_ref=Wp.at[:, part(-dy, 1, height, 1), part(-dx, EDGE, width, EDGE)],
+            src_ref=src,
+            dst_ref=dst,
             send_sem=rim_send.at[s],
             recv_sem=rim_recv.at[s],
             device_id=at(dy, dx),
             device_id_type=MESH,
         )
 
-    def cell_copy(s):
+    def border_unpack(s):
+        border(s).wait_recv()
         dy, dx = DIRS[s]
-        return pltpu.make_async_remote_copy(
-            src_ref=CW.at[8],
-            dst_ref=CW.at[s],
-            send_sem=cell_send.at[s],
-            recv_sem=cell_recv.at[s],
-            device_id=at(dy, dx),
-            device_id_type=MESH,
-        )
+        if dx != 0:
+            tile = SC[s - 4].astype(F32)
+            for d in range(2):
+                i = 8 * d + (0 if dy < 0 else 7)
+                side_column(d, height + 1 if dy < 0 else 0, 0 if dx < 0 else 1, tile[i : i + 1])
 
     def each(sides, sign, act):
         for s in sides:
@@ -279,45 +391,27 @@
     everywhere = range(8)
 
     def coarse_warp():
-        def push_wait(k, _):
-            push(k).wait_recv()
-            return 0
-
-        lax.fori_loop(1, n, push_wait, 0)
+        each(everywhere, -1, lambda s: list_copy(s).wait_recv())
         every = G[...].reshape(n * 2 * cells, -1)
-        source = lax.broadcasted_iota(jnp.int32, (2 * cells, n * 2 * cells), 1).astype(F32)
-        small = lax.broadcasted_iota(jnp.int32, (cells, cells), 0) == lax.broadcasted_iota(
-            jnp.int32, (cells, cells), 1
-        )
-        warped = jnp.zeros((2 * cells, feat), F32)
+        source = lax.broadcasted_iota(jnp.int32, (9 * 2 * cells, n * 2 * cells), 1).astype(F32)
+        columns = LB[...].reshape(9 * 8, 128).T[:cells]
+        warped = jnp.zeros((9 * 2 * cells, feat), F32)
         for e in range(2):
-            names, shares = [], []
-            for d in range(2):
-                base = tiles[d, 0, 0, e] * (2 * cells) + (1 - d) * cells
-                row = (pixel[d, e] + base).astype(F32)
-                names.append(jnp.sum(jnp.where(small, row, 0.0), axis=1, keepdims=True))
-                row = weight[d, 0][e : e + 1].astype(F32)
-                shares.append(jnp.sum(jnp.where(small, row, 0.0), axis=1, keepdims=True))
-            names, shares = jnp.concatenate(names, axis=0), jnp.concatenate(shares, axis=0)
+            at_lane = [8 * slot + 2 * d + e for slot in range(9) for d in range(2)]
+            names = jnp.concatenate([columns[:, i : i + 1] for i in at_lane], axis=0)
+            shares = jnp.concatenate([columns[:, i + 4 : i + 5] for i in at_lane], axis=0)
             chosen = jnp.where(source == names, shares, 0.0).astype(BF)
             warped = warped + jnp.dot(chosen, every, preferred_element_type=F32)
-        CW[8] = warped.astype(BF)
-        for s, (dy, dx) in enumerate(DIRS):
-            @pl.when(jnp.logical_not(has(-dy, -dx)))
-            def _():
-                CW[s] = jnp.zeros(CW.shape[1:], BF)
-
-        each(everywhere, 1, lambda s: cell_copy(s).start())
+        CW[...] = warped.astype(BF).reshape(9, 2 * cells, feat)
 
     def coarse_flow():
-        each(everywhere, -1, lambda s: cell_copy(s).wait_recv())
         summed = jnp.zeros((2 * cells, feat), F32)
         for dy in (-1, 0, 1):
             own, other = {}, {}
             for dx in (-1, 0, 1):
                 oy, ox = at(dy, dx)
                 there = has(dy, dx)
-                own[dx] = jnp.where(there, G[oy * n_tx + ox].astype(F32), 0.0)
+                own[dx] = jnp.where(there, G[slot_of((oy, ox))].astype(F32), 0.0)
                 slot = 8 if dy == 0 and dx == 0 else DIRS.index((-dy, -dx))
                 other[dx] = CW[slot].astype(F32)
             columns = []
@@ -376,24 +470,33 @@
         two = 1 - ty
         halo_wait(across)
         loop(height + MARGIN, MARGIN * one, shift)
+        hand_on(1)
+        warp(one)
+        side_pack(one, 0)
+        each(across, 1, lambda s: side(s, 0).start())
         loop(height + 1, one, functools.partial(spread, 0))
-        warp(one)
-        each(across, 1, lambda s: side(s, one, 0).start())
-        coarse_warp()
-        each(across, -1, lambda s: side(s, one, 0).wait_recv())
+        each(across, -1, lambda s: side_unpack(s, one, 0))
         loop(9, 9 * one, functools.partial(spread, 1))
+        hand_on(2)
         conv(10 * one, 3)
+        hand_on(3)
         halo_wait(along)
         loop(MARGIN, (height + MARGIN) * two, shift)
+        warp(two)
+        side_pack(two, 1)
+        each(across, 1, lambda s: side(s, 1).start())
+        each(along, 1, lambda s: border(s).start())
+        hand_on(4)
         spread(0, (height + 1) * two)
-        warp(two)
-        each(along, 1, lambda s: border(s).start())
-        each(across, 1, lambda s: side(s, two, 1).start())
+        each(across, -1, lambda s: side_unpack(s, two, 1))
+        loop(8, 1 + 8 * two, functools.partial(spread, 1))
+        conv(2 + 4 * two, 2)
+        for j in range(5, len(steps) + 1):
+            hand_on(j)
+        coarse_warp()
         ups = coarse_flow()
-        each(across, -1, lambda s: side(s, two, 1).wait_recv())
-        loop(8, 1 + 8 * two, functools.partial(spread, 1))
-        conv(2 + 4 * two, 4)
-        each(along, -1, lambda s: border(s).wait_recv())
+        conv(6 + 4 * two, 2)
+        each(along, -1, border_unpack)
         spread(1, (height + 1) * two)
         conv(14 * two, 1)
     else:
@@ -403,14 +506,18 @@
         loop(height + 2, 0, functools.partial(spread, 0))
         warp(0)
         warp(1)
+        side_pack(0, 0)
+        each(across, 1, lambda s: side(s, 0).start())
+        side_pack(1, 1)
+        each(across, 1, lambda s: side(s, 1).start())
         each(along, 1, lambda s: border(s).start())
-        each(across, 1, lambda s: side(s, 0, 0).start())
-        each(across, 1, lambda s: side(s, 1, 1).start())
+        for j in range(1, len(steps) + 1):
+            hand_on(j)
         coarse_warp()
         ups = coarse_flow()
-        each(along, -1, lambda s: border(s).wait_recv())
-        each(across, -1, lambda s: side(s, 0, 0).wait_recv())
-        each(across, -1, lambda s: side(s, 1, 1).wait_recv())
+        each(along, -1, border_unpack)
+        each(across, -1, lambda s: side_unpack(s, 0, 0))
+        each(across, -1, lambda s: side_unpack(s, 1, 1))
         loop(height + 2, 0, functools.partial(spread, 1))
         conv(0, 4)
         conv(8, 4)
@@ -419,18 +526,14 @@
         for k in range(2):
             out[d, k] = out[d, k] + (ups[d][k : k + 1] + out_b[k])
 
-    for f in range(2):
-        each(everywhere, 1, lambda s: halo(s, f).wait_send())
+    each(everywhere, 1, lambda s: halo(s).wait_send())
     each(along, 1, lambda s: border(s).wait_send())
-    each(across, 1, lambda s: side(s, one, 0).wait_send())
-    each(across, 1, lambda s: side(s, two, 1).wait_send())
-    each(everywhere, 1, lambda s: cell_copy(s).wait_send())
-
-    def push_done(k, _):
-        push(k).wait_send()
-        return 0
-
-    lax.fori_loop(1, n, push_done, 0)
+    each(across, 1, lambda s: side(s, 0).wait_send())
+    each(across, 1, lambda s: side(s, 1).wait_send())
+    each(everywhere, 1, lambda s: list_copy(s).wait_send())
+
+    for j in range(len(steps)):
+        hand(j).wait_send()
 
 
 def on_device(
@@ -440,6 +543,7 @@
     height, width, feat = frame_zero.shape
     cells = width // POOL
     n = n_ty * n_tx
+    steps = max(n.bit_length() - 1, 1)
     vmem = pl.BlockSpec(memory_space=pltpu.VMEM)
     smem = pl.BlockSpec(memory_space=pltpu.SMEM)
     hbm = pl.BlockSpec(memory_space=pl.ANY)
@@ -457,6 +561,13 @@
             pltpu.VMEM((n, 2 * cells, feat), BF),
             pltpu.VMEM((9, 2 * cells, feat), BF),
             pltpu.VMEM((4, 6, 8, 128), F32),
+            pltpu.VMEM((9, 8, 128), F32),
+            pltpu.VMEM((2, 2, height * MARGIN, feat), BF),
+            pltpu.VMEM((2, 2, height * MARGIN, feat), BF),
+            pltpu.VMEM((4, 2, 16, feat), BF),
+            pltpu.VMEM((2, 2, 16, feat), BF),
+            pltpu.VMEM((2, 2, 16, feat), BF),
+            pltpu.VMEM((4, 16, feat), BF),
             pltpu.VMEM(offset_whole.shape, jnp.int32),
             pltpu.VMEM(offset_frac.shape, F32),
             pltpu.VMEM(list_pixel.shape, jnp.int32),
@@ -466,7 +577,7 @@
             pltpu.VMEM((1, feat), F32),
             pltpu.VMEM((1, feat), F32),
             pltpu.VMEM((2, feat), BF),
-            dma((13,)), dma((8, 2)), dma((8, 2)), dma((n,)), dma((n,)),
+            dma((13,)), dma((8,)), dma((8,)), dma((steps,)), dma((steps,)),
             dma((8,)), dma((8,)), dma((8, 2)), dma((8, 2)), dma((8,)), dma((8,)),
         ],
         compiler_params=pltpu.CompilerParams(

time: 35.3 us -> 28.4 us (0.80)
  the two profiles are of different devices: /device:TPU:1 before, /device:TPU:0 now
where the time goes in v3:
time: 28.4 us; the launch traced here: 28.2 us
  Pallas kernels  26.8 us (94%)
  local copies, waits for them, and re-layouts  1.38 us (5%)
    pallas_call x1, Pallas kernels, on_device(): pl.pallas_call(functools.partial(kernel, n_ty, n_tx, height, width), out_...  26.8 us
    unnamed x1, local copies, waits for them, and re-layouts  1.38 us

profile of v3, /device:TPU:0, one launch (start us, length us, event | category | flops | bytes accessed | tf_op | source)
XLA Modules:
  0.0 28.2 jit_solution(3997868493537974406)
XLA Ops:
  0.0 26.8 %shard_map.127 = f32[2,2,16,128]{3,2,1,0:T(8,128)} custom-call(bf16[16,128,128]{2,1,0:T(8,128)(2,1)} %f0.1, bf16[16,128,128]{2,1,0:T(8,128)(2,1)} %f1.1, s32[2,2,16,128]{3,2,1,0:T(8,128)} %whole_in.1, f32[2,2,16,128]{3,2,1,0:T(8,128)} %frac_in.1, s32[2,1,1,2]{3,2,1,0:T(1,128)} %bitcast.11, s32[2,2,1,8]{3,2,1,0:T(1,128)} %pixel_in.1, ...), custom_call_target="tpu_custom_call" | custom-call | tf_op jit(solution)/shard_map/pallas_call | solution.py:551
  26.8 1.4 %copy.17 = f32[2,2,16,128]{3,2,1,0:T(8,128)} copy(f32[2,2,16,128]{3,2,1,0:T(8,128)} %shard_map.127) | data formatting | bytes 65536
